TPU v7x, 256 devices: a whole 4x4x8 slice. The times are simulated.
256 devices in a mesh: inst: 4 (over x_lo, core), space: 64 (over x_hi, z, y).
Axes of the slice: x: 4 (x_hi: 2, x_lo: 2; x = x_hi * 2 + x_lo), y: 4, z: 8, core: 2. Of those that a mesh axis runs over, the one named last changes fastest.
Arguments:
- flow_state: float32 [8, 5, 4096, 256], P('inst', None, 'space'), may hold values from -6 to 6
- flow_source: float32 [8, 5, 4096, 256], P('inst', None, 'space'), may hold values from -6 to 6
- pseudo_step: float32 [4096, 256], P('space'), may hold values from 0.03 to 0.12
- flux_jacobian: float32 [5, 5], replicated, may hold values from -2.5 to 2.5
- stator_donor: int32 [8, 4096], P('inst', 'space'), may hold values from 0 to 4095, as said below
- stator_weight: float32 [8, 4096], P('inst', 'space'), may hold values from 0 to 1
- rotor_donor: int32 [8, 4096], P('inst', 'space'), may hold values from 0 to 4095, as said below
- rotor_weight: float32 [8, 4096], P('inst', 'space'), may hold values from 0 to 1
Outputs:
- new_state: float32 [8, 5, 4096, 256], P('inst', None, 'space')
- residual: float32 [8, 5, 4096, 256], P('inst', None, 'space')
Inputs may be any that keep to these rules, and one draw needn't show every extreme that they name: `stator_donor`: for each instance n the row holds the rotation j -> (j - shift_n) mod 4096 of the rows, so entry j is (j - stator_shift_n) mod 4096, where stator_shift_n is a shift of its own for each instance. `rotor_donor`: for each instance n the row holds the rotation j -> (j + shift_n) mod 4096 of the rows, so entry j is (j + rotor_shift_n) mod 4096, where rotor_shift_n is a shift of its own for each instance, independent of stator_shift_n.
All inputs are finite; a program needn't handle non-finite values.
Results may differ from a plain program's by a relative error of at most 0.0001.
Values sent between devices are 32-bit elements; how exact they have to be, the bound alone decides.
A program may use at most 128 MiB of HBM per device.

v0:
```python
import math

import jax
import jax.numpy as jnp
from jax import lax
from jax.sharding import PartitionSpec as P

NT = 8
SWEEPS = 2


viscosity = 0.5


def with_halo(x, sides, width):
    for axis, dim in sides:
        count, length = (lax.axis_size(axis), x.shape[dim])
        up = [(i, (i + 1) % count) for i in range(count)]
        down = [(j, i) for i, j in up]
        last = lax.slice_in_dim(x, length - width, length, axis=dim)
        leading = lax.slice_in_dim(x, 0, width, axis=dim)
        before = lax.ppermute(last, axis, up)
        after = lax.ppermute(leading, axis, down)
        x = jnp.concatenate([before, x, after], axis=dim)
    return x


def spectral_table(count):
    rows = jnp.arange(count, dtype=jnp.int32)[:, None]
    columns = jnp.arange(count, dtype=jnp.int32)[None, :]
    gap = rows - columns
    parity = (1 - 2 * (gap % 2)).astype(jnp.float32)
    angle = math.pi / count * gap.astype(jnp.float32)
    sine = jnp.where(gap == 0, jnp.float32(1.0), jnp.sin(angle))
    value = 0.5 * parity * jnp.cos(angle) / sine
    return jnp.where(gap == 0, jnp.float32(0.0), value)


def interpolate(column, donor, weight):
    total = column.shape[2]
    first = jnp.take_along_axis(column, donor[:, None, :], axis=2)
    second = jnp.take_along_axis(column, ((donor + 1) % total)[:, None, :], axis=2)
    return (1.0 - weight)[:, None, :] * first + weight[:, None, :] * second


def spatial(flow, upper, lower, stator_in, rotor_in, flux_jacobian):
    half = flow.shape[3] // 2
    zero_col = jnp.zeros(flow.shape[:3] + (1,), jnp.float32)
    left_cells = jnp.concatenate([zero_col, flow[..., :-1]], axis=3).at[..., half].set(stator_in)
    right_cells = jnp.concatenate([flow[..., 1:], zero_col], axis=3).at[..., half - 1].set(rotor_in)
    convect = jnp.einsum(
        "vw,nwca->nvca", flux_jacobian, flow - left_cells, precision=lax.Precision.HIGHEST
    )
    return convect + viscosity * (4.0 * flow - left_cells - right_cells - upper - lower)


def apply_columns(local_rows, piece):
    return jnp.einsum("nm,mvca->nvca", local_rows, piece, precision=lax.Precision.HIGHEST)


def local(
    flow_state,
    flow_source,
    pseudo_step,
    flux_jacobian,
    stator_donor,
    stator_weight,
    rotor_donor,
    rotor_weight,
):
    local_count = flow_state.shape[0]
    position = lax.axis_index("inst")
    table = spectral_table(NT)
    half = flow_state.shape[3] // 2
    local_rows = lax.dynamic_slice_in_dim(table, position * local_count, local_count, 0)
    flow = flow_state
    residual = flow
    for sweep in range(SWEEPS):
        rotor_all, stator_all = (
            lax.all_gather(flow[..., half - 1], "space", axis=2, tiled=True),
            lax.all_gather(flow[..., half], "space", axis=2, tiled=True),
        )
        stator_in = interpolate(rotor_all, stator_donor, stator_weight)
        rotor_in = interpolate(stator_all, rotor_donor, rotor_weight)
        padded = with_halo(flow, (("space", 2),), 1)
        upper = padded[:, :, :-2]
        lower = padded[:, :, 2:]
        derivative = apply_columns(local_rows, lax.all_gather(flow, "inst", axis=0, tiled=True))
        residual = (
            spatial(flow, upper, lower, stator_in, rotor_in, flux_jacobian)
            + derivative
            - flow_source
        )
        flow = flow - pseudo_step[None, None] * residual
    return (flow, residual)


def solution(mesh):
    return jax.shard_map(
        local,
        mesh=mesh,
        in_specs=(
            P("inst", None, "space", None),
            P("inst", None, "space", None),
            P("space", None),
            P(),
            P("inst", "space"),
            P("inst", "space"),
            P("inst", "space"),
            P("inst", "space"),
        ),
        out_specs=(P("inst", None, "space", None), P("inst", None, "space", None)),
        check_vma=False,
    )
```

profile of v0, /device:TPU:2, one launch (start us, length us, event | category | flops | bytes accessed | tf_op | source)
XLA Modules:
  0.0 1456.3 jit_solution(14926466707886030366)
XLA Ops:
  7.2 0.0 copy-start
  7.2 0.0 all-gather.7.cloned.1.call-start
  7.2 0.7 all-gather.7.cloned.1.call-update
  7.9 0.0 all-gather.9.cloned.1.call-start
  8.0 1.5 copy.116
  9.5 1.7 collective-permute-start
  11.2 8.4 collective-permute-start.1
  19.5 1.2 fusion.59
  20.8 0.9 copy.137
  21.6 0.7 bitcast_or_fusion.3
  22.3 0.1 reshape.275
  22.4 212.2 %all-gather = f32[2,5,4096,1]{1,2,0,3:T(8,128)} all-gather(f32[2,5,64,1]{1,2,0,3:T(8,128)S(1)} %copy.137), channel_id=2, replica_groups=mesh['inst'=4,'space'=64] {'space'}, dimensions={2}, use_global_device_ids=true | all-gather | bytes 166400 | tf_op jit(solution)/shard_map/all_gather | solution.py:80
  234.6 1.8 gather_fusion.1
  236.4 0.1 copy.100
  236.4 0.1 reshape.270
  236.5 1.8 gather_fusion
  238.3 0.1 copy.99
  238.4 0.3 copy.101
  238.7 0.9 copy.138
  239.6 0.1 reshape.280
  239.7 210.2 %all-gather.1 = f32[2,5,4096,1]{1,2,0,3:T(8,128)} all-gather(f32[2,5,64,1]{1,2,0,3:T(8,128)S(1)} %copy.138), channel_id=3, replica_groups=mesh['inst'=4,'space'=64] {'space'}, dimensions={2}, use_global_device_ids=true | all-gather | bytes 166400 | tf_op jit(solution)/shard_map/all_gather | solution.py:81
  449.9 1.8 gather_fusion.2
  451.7 0.1 copy.106
  451.8 0.1 reshape.285
  451.9 1.8 gather_fusion.3
  453.6 0.1 copy.107
  453.8 1.0 copy.108
  454.8 0.3 fusion.57
  455.2 0.3 concatenate.34
  455.5 1.0 concatenate.35
  456.6 1.8 scatter.14
  458.4 12.3 scatter.15
  470.7 0.0 all-gather.7.cloned.1.call-done
  470.7 5.3 fusion.2
  476.1 3.9 fusion.5
  480.0 1.0 copy.129
  481.1 0.0 all-gather.9.cloned.1.call-update
  481.1 0.2 fusion.54
  481.3 446.8 %all-gather.2 = f32[2,5,4096,1]{3,1,2,0:T(8,128)} all-gather(f32[2,5,64,1]{3,1,2,0:T(8,128)S(1)} %get-tuple-element.59), channel_id=4, replica_groups=mesh['inst'=4,'space'=64] {'space'}, dimensions={2}, use_global_device_ids=true | all-gather | bytes 166400 | tf_op jit(solution)/shard_map/all_gather | solution.py:80
  928.1 17.8 %copy.117 = f32[2,5,4096,1]{2,0,1,3:T(2,128)S(1)} copy(f32[2,5,4096,1]{3,1,2,0:T(8,128)} %all-gather.2) | data formatting | bytes 327680 | tf_op jit(solution)/shard_map/all_gather | solution.py:80
  945.8 2.7 copy.118
  948.5 1.8 gather_fusion.4
  950.3 1.8 gather_fusion.5
  952.1 434.6 %all-gather.3 = f32[2,5,4096,1]{3,1,2,0:T(8,128)} all-gather(f32[2,5,64,1]{3,1,2,0:T(8,128)S(1)} %get-tuple-element.60), channel_id=5, replica_groups=mesh['inst'=4,'space'=64] {'space'}, dimensions={2}, use_global_device_ids=true | all-gather | bytes 166400 | tf_op jit(solution)/shard_map/all_gather | solution.py:81
  1386.7 17.8 %copy.123 = f32[2,5,4096,1]{2,0,1,3:T(2,128)S(1)} copy(f32[2,5,4096,1]{3,1,2,0:T(8,128)} %all-gather.3) | data formatting | bytes 327680 | tf_op jit(solution)/shard_map/all_gather | solution.py:81
  1404.5 2.7 copy.124
  1407.1 1.8 gather_fusion.6
  1408.9 1.8 gather_fusion.7
  1410.7 0.1 copy.119
  1410.8 0.1 copy.121
  1410.9 0.3 copy.122
  1411.1 1.3 fusion.55
  1412.5 0.3 concatenate.38
  1412.8 0.1 copy.125
  1412.9 0.1 copy.127
  1413.0 1.0 copy.128
  1414.0 2.3 concatenate.39
  1416.3 7.7 collective-permute-start.3
  1424.1 1.8 scatter.16
  1425.9 12.3 scatter.19
  1438.2 5.3 fusion
  1443.5 3.9 multiply_subtract_fusion
  1447.4 1.0 copy.133
  1448.4 1.0 copy.134
  (35 shorter events, 0.2 us)
Async XLA Ops:
  7.2 468.9 %copy-start = (f32[5,5]{1,0:T(8,128)S(1)}, f32[5,5]{1,0:T(8,128)}, u32[]{:S(2)}) copy-start(f32[5,5]{1,0:T(8,128)} %param.21) | copy-start | bytes 304
  7.2 463.6 %all-gather.7.cloned.1.call-start = ((), (), s32[]{:S(2)}) async-start(), calls=%async_computation | async-start | bytes 3276800 | tf_op jit(solution)/shard_map/all_gather | solution.py:88
  7.9 230.5 %copy-start.7 = (s32[2,64]{1,0:T(2,128)S(1)}, s32[2,64]{1,0:T(2,128)}, u32[]{:S(2)}) copy-start(s32[2,64]{1,0:T(2,128)} %param.22) | copy-start | bytes 1540
  7.9 230.5 %copy-start.5 = (f32[2,64]{1,0:T(2,128)S(1)}, f32[2,64]{1,0:T(2,128)}, u32[]{:S(2)}) copy-start(f32[2,64]{1,0:T(2,128)} %param.23) | copy-start | bytes 1540
  7.9 231.6 %copy-start.8 = (s32[2,64]{1,0:T(2,128)S(1)}, s32[2,64]{1,0:T(2,128)}, u32[]{:S(2)}) copy-start(s32[2,64]{1,0:T(2,128)} %param.24) | copy-start | bytes 1540
  7.9 1430.2 %all-gather.9.cloned.1.call-start = ((), (), s32[]{:S(2)}) async-start(), calls=%async_computation.1 | async-start | bytes 3276800 | tf_op jit(solution)/shard_map/all_gather | solution.py:88
  9.5 466.5 %collective-permute-start = (f32[2,5,1,256]{3,1,2,0:T(8,128)S(1)}, f32[2,5,1,256]{3,1,2,0:T(8,128)S(1)}, u32[]{:S(2)}, u32[]{:S(2)}) collective-permute-start(f32[2,5,1,256]{3,1,2,0:T(8,128)S(1)} %get-tuple-element.67), channel_id=1, source_target_pairs={{0,1},{1,2},{2,3},{3,4},{4,5},{5,6},{6,7},{7,8},{8,9},{9,10},{10,1... | collective-permute-start | bytes 30728 | tf_op jit(solution)/shard_map/ppermute | solution.py:22
  11.2 464.9 %collective-permute-start.1 = (f32[2,5,1,256]{3,1,2,0:T(8,128)S(1)}, f32[2,5,1,256]{3,1,2,0:T(8,128)S(1)}, u32[]{:S(2)}, u32[]{:S(2)}) collective-permute-start(f32[2,5,1,256]{3,1,2,0:T(8,128)S(1)} %get-tuple-element.68), channel_id=1, source_target_pairs={{1,0},{2,1},{3,2},{4,3},{5,4},{6,5},{7,6},{8,7},{9,8},{10,9},{11,1... | collective-permute-start | bytes 30728 | tf_op jit(solution)/shard_map/ppermute | solution.py:23
  22.4 431.3 %copy-start.6 = (f32[2,64]{1,0:T(2,128)S(1)}, f32[2,64]{1,0:T(2,128)}, u32[]{:S(2)}) copy-start(f32[2,64]{1,0:T(2,128)} %param.25) | copy-start | bytes 1540
  455.5 20.6 %copy-start.1 = (f32[2,5,64,256]{3,2,1,0:T(8,128)S(1)}, f32[2,5,64,256]{3,2,1,0:T(8,128)}, u32[]{:S(2)}) copy-start(f32[2,5,64,256]{3,2,1,0:T(8,128)} %param.19) | copy-start | bytes 1966084
  455.5 20.6 %copy-start.4 = (f32[64,256]{1,0:T(8,128)S(1)}, f32[64,256]{1,0:T(8,128)}, u32[]{:S(2)}) copy-start(f32[64,256]{1,0:T(8,128)} %param.20) | copy-start | bytes 196612
  458.3 17.7 %copy-start.3 = (f32[2,5,64,256]{3,1,2,0:T(8,128)}, f32[2,5,64,256]{3,1,2,0:T(8,128)S(1)}, u32[]{:S(2)}) copy-start(f32[2,5,64,256]{3,1,2,0:T(8,128)S(1)} %scatter.14) | copy-start | bytes 1966084
  1416.3 27.2 %collective-permute-start.2 = (f32[2,5,1,256]{3,1,2,0:T(8,128)S(1)}, f32[2,5,1,256]{3,1,2,0:T(8,128)S(1)}, u32[]{:S(2)}, u32[]{:S(2)}) collective-permute-start(f32[2,5,1,256]{3,1,2,0:T(8,128)S(1)} %get-tuple-element.63), channel_id=1, source_target_pairs={{0,1},{1,2},{2,3},{3,4},{4,5},{5,6},{6,7},{7,8},{8,9},{9,10},{10,1... | collective-permute-start | bytes 30728 | tf_op jit(solution)/shard_map/ppermute | solution.py:22
  1416.3 27.2 %collective-permute-start.3 = (f32[2,5,1,256]{3,1,2,0:T(8,128)S(1)}, f32[2,5,1,256]{3,1,2,0:T(8,128)S(1)}, u32[]{:S(2)}, u32[]{:S(2)}) collective-permute-start(f32[2,5,1,256]{3,1,2,0:T(8,128)S(1)} %get-tuple-element.64), channel_id=1, source_target_pairs={{1,0},{2,1},{3,2},{4,3},{5,4},{6,5},{7,6},{8,7},{9,8},{10,9},{11,1... | collective-permute-start | bytes 30728 | tf_op jit(solution)/shard_map/ppermute | solution.py:23
  1425.9 12.3 copy-start.2
Sparse Core Ops, SparseCore 0:
  9.8 37.2 all-gather.6
  481.2 27.5 all-gather.8
where the time goes:
time: 1460 us
  blocking collectives  1300 us (89%)
  local copies, waits for them, and re-layouts  100 us (7%)
  matrix products  18.4 us (1%)
  starting transfers between devices  17.9 us (1%)
    all_gather x2, blocking collectives, local(): lax.all_gather(flow[..., half - 1], 'space', axis=2, tiled=True)  659 us
    all_gather x2, blocking collectives, local(): lax.all_gather(flow[..., half], 'space', axis=2, tiled=True)  645 us
  transfers between devices with their start and end apart: 6, of which 0 were waited for; matrix products, arithmetic and copies ran while one was open for 7% of the time, Pallas kernels for 0%

commit v1 on v0

v1 whole, which is shorter than its diff:
```python
import math

import jax
import jax.numpy as jnp
from jax import lax
from jax.experimental import pallas as pl
from jax.experimental.pallas import tpu as pltpu
from jax.sharding import PartitionSpec as P

MESH = pl.DeviceIdType.MESH
NT = 8
NV = 5
ROWS = 64
AX = 256
LANES = 128
CHUNK = 8
CHUNKS = ROWS // CHUNK
SX, SZ, SY = 2, 8, 4
SPACE = SX * SZ * SY
PLANE = SX * SY
VISCOSITY = 0.5


def spectral(gap):
    gap = gap % NT
    if gap == 0:
        return 0.0
    return 0.5 * (-1.0) ** gap * math.cos(math.pi * gap / NT) / math.sin(math.pi * gap / NT)


def kernel(
    flow_hbm, source_hbm, step_hbm, jac, stator_donor, stator_weight, rotor_donor, rotor_weight,
    state_hbm, resid_hbm,
    flow0, flow1, source, step, sib0, sib1, send0, send1, recv0, recv1, out_state, out_resid,
    corner, plane0, plane1, ring0, ring1, inflow,
    load_sem, out_sem, sib_ssem, sib_rsem, par_ssem, par_rsem, halo_ssem, halo_rsem,
    plane_ssem, plane_rsem, ring_ssem, ring_rsem,
):
    inst, space = lax.axis_index("inst"), lax.axis_index("space")
    pair, core = inst // 2, inst % 2
    x, z, y = space // (SZ * SY), (space // SY) % SZ, space % SY
    sibling = (pair * 2 + 1 - core, space)
    partner = ((1 - pair) * 2 + core, space)
    above = (inst, (space + SPACE - 1) % SPACE)
    below = (inst, (space + 1) % SPACE)
    slot = x * SY + y
    planes, rings = (plane0, plane1), (ring0, ring1)

    def plane_peer(k):
        other = (slot + k) % PLANE
        return other, (inst, (other // SY) * (SZ * SY) + z * SY + other % SY)

    def ring_peer(k):
        other = (z + k) % SZ
        return other, (inst, x * (SZ * SY) + other * SY + y)

    flow_in = pltpu.make_async_copy(flow_hbm, flow0.at[:, :, pl.ds(CHUNK, ROWS), :], load_sem.at[0])
    source_in = pltpu.make_async_copy(source_hbm, source, load_sem.at[1])
    step_in = pltpu.make_async_copy(step_hbm, step, load_sem.at[2])
    flow_in.start()
    source_in.start()
    step_in.start()

    barrier = pltpu.get_barrier_semaphore()
    greeted = [sibling, partner, above, below]
    greeted += [plane_peer(k)[1] for k in range(1, PLANE)]
    greeted += [ring_peer(k)[1] for k in range(1, SZ)]
    for device in greeted:
        pl.semaphore_signal(barrier, inc=1, device_id=device, device_id_type=MESH)

    lane = lax.broadcasted_iota(jnp.int32, (CHUNK, LANES), 1)
    low = lane < ROWS

    def scalars(table):
        return [[table(a - b) for b in range(2)] for a in range(2)]

    from_own = scalars(spectral)
    from_sib = scalars(lambda g: jnp.where(core == 0, spectral(g - 2), spectral(g + 2)).astype(jnp.float32))
    to_own = scalars(lambda g: spectral(g + 4))
    to_sib = scalars(lambda g: jnp.where(core == 0, spectral(g + 2), spectral(g + 6)).astype(jnp.float32))

    def remote(src, dst, ssem, rsem, device):
        return pltpu.make_async_remote_copy(
            src_ref=src, dst_ref=dst, send_sem=ssem, recv_sem=rsem, device_id=device, device_id_type=MESH
        )

    def rows_at(g):
        return pl.ds(pl.multiple_of(CHUNK + g * CHUNK, CHUNK), CHUNK)

    def sib_copy(sweep, g):
        flow, sib = (flow0, sib0) if sweep == 0 else (flow1, sib1)
        at = sweep * CHUNKS + g
        return remote(flow.at[:, :, rows_at(g), :], sib.at[g], sib_ssem.at[at], sib_rsem.at[at], sibling)

    def par_copy(sweep, g):
        send, recv = (send0, recv0) if sweep == 0 else (send1, recv1)
        at = sweep * CHUNKS + g
        return remote(send.at[g], recv.at[g], par_ssem.at[at], par_rsem.at[at], partner)

    def halo_copies(sweep):
        flow = flow0 if sweep == 0 else flow1
        first = flow.at[:, :, pl.ds(CHUNK, 1), :]
        last = flow.at[:, :, pl.ds(CHUNK + ROWS - 1, 1), :]
        before = flow.at[:, :, pl.ds(CHUNK - 1, 1), :]
        after = flow.at[:, :, pl.ds(CHUNK + ROWS, 1), :]
        up, down = 2 * sweep, 2 * sweep + 1
        return (
            remote(first, after, halo_ssem.at[up], halo_rsem.at[up], above),
            remote(last, before, halo_ssem.at[down], halo_rsem.at[down], below),
        )

    def plane_copy(sweep, k):
        _, device = plane_peer(k)
        mine = planes[sweep].at[slot]
        return remote(mine, mine, plane_ssem.at[sweep * PLANE + k], plane_rsem.at[sweep * PLANE + slot], device)

    def plane_arrival(sweep, k):
        other, device = plane_peer(k)
        theirs = planes[sweep].at[other]
        return remote(theirs, theirs, plane_ssem.at[sweep * PLANE + k], plane_rsem.at[sweep * PLANE + other], device)

    def ring_copy(sweep, k):
        _, device = ring_peer(k)
        mine = rings[sweep].at[z]
        return remote(mine, mine, ring_ssem.at[sweep * SZ + k], ring_rsem.at[sweep * SZ + z], device)

    def ring_arrival(sweep, k):
        other, device = ring_peer(k)
        theirs = rings[sweep].at[other]
        return remote(theirs, theirs, ring_ssem.at[sweep * SZ + k], ring_rsem.at[sweep * SZ + other], device)

    def extract(sweep):
        flow = flow0 if sweep == 0 else flow1

        def body(g, _):
            for n in range(2):
                total = jnp.zeros((CHUNK, LANES), jnp.float32)
                for c in range(2):
                    for v in range(NV):
                        tile = flow[n, v, rows_at(g), pl.ds(c * LANES, LANES)]
                        q = c * CHUNK + v
                        turned = pltpu.roll(tile, (q + 1) if c == 0 else q, axis=1)
                        total = jnp.where(lane == q, turned, total)
                corner[pl.ds(pl.multiple_of(n * ROWS + g * CHUNK, CHUNK), CHUNK), :] = total
            return 0

        lax.fori_loop(0, CHUNKS, body, 0)
        planes[sweep][slot] = corner[...].T[0 : 2 * CHUNK, :]

    def donor(c, n):
        return (stator_donor if c == 0 else rotor_donor)[n, 0]

    def forward(sweep):
        for c in range(2):
            for n in range(2):
                ahead = (donor(c, n) // ROWS + SPACE - space) % SPACE
                halves = []
                for d in (ahead, (ahead + 1) % SPACE):
                    dx, dz, dy = d // (SZ * SY), (d // SY) % SZ, d % SY
                    carry = (y + dy) // SY
                    wants = (z + 2 * SZ - dz - carry) % SZ
                    over = (wants + dz + carry) // SZ
                    pick = ((x + dx + over) % SX) * SY + (y + dy) % SY
                    halves.append(planes[sweep][pick, pl.ds(c * CHUNK, CHUNK), :])
                first, second = halves
                if n == 0:
                    both = jnp.where(low, first, pltpu.roll(second, ROWS, axis=1))
                else:
                    both = jnp.where(low, pltpu.roll(first, ROWS, axis=1), second)
                rings[sweep][z, pl.ds((c * 2 + n) * CHUNK, CHUNK), :] = both

    def interpolate(sweep):
        corner[...] = jnp.zeros_like(corner)
        for c in range(2):
            weights = stator_weight if c == 0 else rotor_weight
            for n in range(2):
                start = donor(c, n)
                block = start // ROWS
                group = pl.ds((c * 2 + n) * CHUNK, CHUNK)
                here = rings[sweep][(block // SY) % SZ, group, :]
                there = rings[sweep][((block + 1) // SY) % SZ, group, :]
                window = jnp.where(low, here, there)
                offset = start % ROWS
                first = pltpu.roll(window, (LANES - offset) % LANES, axis=1)
                second = pltpu.roll(window, LANES - 1 - offset, axis=1)
                weight = weights[pl.ds(n, 1), :]
                weight = jnp.concatenate([weight, weight], axis=1)
                corner[group, :] = (1.0 - weight) * first + weight * second
        inflow[...] = corner[...].T[0:ROWS, :]

    def mix(sweep, g):
        flow, sib, send = (flow0, sib0, send0) if sweep == 0 else (flow1, sib1, send1)
        for v in range(NV):
            for t in range(2):
                at = pl.ds(t * LANES, LANES)
                own = [flow[n, v, rows_at(g), at] for n in range(2)]
                other = [sib[g, n, v, :, at] for n in range(2)]
                for a in range(2):
                    send[g, a, v, :, at] = (
                        to_own[a][0] * own[0] + to_own[a][1] * own[1]
                        + (to_sib[a][0] * other[0] + to_sib[a][1] * other[1])
                    )

    jacobian = [[jac[v, w] for w in range(NV)] for v in range(NV)]

    def advance(sweep, g):
        flow, sib, recv = (flow0, sib0, recv0) if sweep == 0 else (flow1, sib1, recv1)
        here = pl.ds(pl.multiple_of(g * CHUNK, CHUNK), CHUNK)
        entering = inflow[here, :]
        for t in range(2):
            at = pl.ds(t * LANES, LANES)
            pace = step[here, at]
            centre = []
            for n in range(2):
                centre.append([flow[n, v, rows_at(g), at] for v in range(NV)])
            for n in range(2):
                diff, smooth = [], []
                for v in range(NV):
                    window = flow[n, v, pl.ds(pl.multiple_of(g * CHUNK, CHUNK), 3 * CHUNK), at]
                    upper = window[CHUNK - 1 : 2 * CHUNK - 1]
                    lower = window[CHUNK + 1 : 2 * CHUNK + 1]
                    f = centre[n][v]
                    left, right = pltpu.roll(f, 1, axis=1), pltpu.roll(f, LANES - 1, axis=1)
                    q = (1 - t) * 2 * CHUNK + n * CHUNK + v
                    if t == 0:
                        q = 2 * CHUNK + n * CHUNK + v
                        left = jnp.where(lane == 0, 0.0, left)
                        right = jnp.where(lane == LANES - 1, pltpu.roll(entering, LANES - 1 - q, axis=1), right)
                    else:
                        q = n * CHUNK + v
                        left = jnp.where(lane == 0, pltpu.roll(entering, (LANES - q) % LANES, axis=1), left)
                        right = jnp.where(lane == LANES - 1, 0.0, right)
                    diff.append(f - left)
                    smooth.append(VISCOSITY * (4.0 * f - left - right - upper - lower))
                for v in range(NV):
                    convect = jacobian[v][0] * diff[0]
                    for w in range(1, NV):
                        convect = convect + jacobian[v][w] * diff[w]
                    derivative = (
                        from_own[n][0] * centre[0][v] + from_own[n][1] * centre[1][v]
                        + (from_sib[n][0] * sib[g, 0, v, :, at] + from_sib[n][1] * sib[g, 1, v, :, at])
                        + recv[g, n, v, :, at]
                    )
                    residual = convect + smooth[v] + derivative - source[n, v, here, at]
                    new = centre[n][v] - pace * residual
                    if sweep == 0:
                        flow1[n, v, rows_at(g), at] = new
                    else:
                        out_state[g, n, v, :, at] = new
                        out_resid[g, n, v, :, at] = residual

    def loop(body):
        def wrapped(g, carry):
            body(g)
            return carry

        lax.fori_loop(0, CHUNKS, wrapped, 0)

    def out_copies(g):
        here = pl.ds(pl.multiple_of(g * CHUNK, CHUNK), CHUNK)
        return (
            pltpu.make_async_copy(out_state.at[g], state_hbm.at[:, :, here, :], out_sem.at[g]),
            pltpu.make_async_copy(out_resid.at[g], resid_hbm.at[:, :, here, :], out_sem.at[CHUNKS + g]),
        )

    flow_in.wait()
    extract(0)
    pl.semaphore_wait(barrier, len(greeted))

    def start_sib(g):
        sib_copy(0, g).start()

    loop(start_sib)
    for k in range(1, PLANE):
        plane_copy(0, k).start()
    for copy in halo_copies(0):
        copy.start()

    def first_mix(g):
        sib_copy(0, g).wait_recv()
        mix(0, g)
        par_copy(0, g).start()

    loop(first_mix)

    def interface(sweep):
        for k in range(1, PLANE):
            plane_arrival(sweep, k).wait_recv()
        forward(sweep)
        for k in range(1, SZ):
            ring_copy(sweep, k).start()
        for k in range(1, SZ):
            ring_arrival(sweep, k).wait_recv()
        interpolate(sweep)

    interface(0)
    for copy in halo_copies(0):
        copy.wait_recv()
    source_in.wait()
    step_in.wait()

    def second_mix(g):
        sib_copy(1, g).wait_recv()
        mix(1, g)
        par_copy(1, g).start()

    def first_sweep(g):
        par_copy(0, g).wait_recv()
        advance(0, g)
        sib_copy(1, g).start()

        @pl.when(g > 0)
        def _():
            second_mix(g - 1)

    loop(first_sweep)
    for copy in halo_copies(1):
        copy.start()
    extract(1)
    for k in range(1, PLANE):
        plane_copy(1, k).start()
    second_mix(CHUNKS - 1)
    interface(1)
    for copy in halo_copies(1):
        copy.wait_recv()

    def second_sweep(g):
        par_copy(1, g).wait_recv()
        advance(1, g)
        for copy in out_copies(g):
            copy.start()

    loop(second_sweep)

    def finish(g):
        for sweep in range(2):
            sib_copy(sweep, g).wait_send()
            par_copy(sweep, g).wait_send()
        for copy in out_copies(g):
            copy.wait()

    loop(finish)
    for sweep in range(2):
        for copy in halo_copies(sweep):
            copy.wait_send()
        for k in range(1, PLANE):
            plane_copy(sweep, k).wait_send()
        for k in range(1, SZ):
            ring_copy(sweep, k).wait_send()


def local(flow_state, flow_source, pseudo_step, flux_jacobian, stator_donor, stator_weight, rotor_donor, rotor_weight):
    f32 = jnp.float32
    block = (2, NV, ROWS, AX)
    padded = (2, NV, ROWS + 2 * CHUNK, AX)
    chunked = (CHUNKS, 2, NV, CHUNK, AX)
    anywhere = pl.BlockSpec(memory_space=pl.ANY)
    smem = pl.BlockSpec(memory_space=pltpu.SMEM)
    vmem = pl.BlockSpec(memory_space=pltpu.VMEM)
    dma = pltpu.SemaphoreType.DMA
    return pl.pallas_call(
        kernel,
        out_shape=(jax.ShapeDtypeStruct(block, f32), jax.ShapeDtypeStruct(block, f32)),
        in_specs=[anywhere, anywhere, anywhere, smem, smem, vmem, smem, vmem],
        out_specs=(anywhere, anywhere),
        scratch_shapes=[
            pltpu.VMEM(padded, f32),
            pltpu.VMEM(padded, f32),
            pltpu.VMEM(block, f32),
            pltpu.VMEM((ROWS, AX), f32),
            *[pltpu.VMEM(chunked, f32) for _ in range(8)],
            pltpu.VMEM((LANES, LANES), f32),
            *[pltpu.VMEM((PLANE, 2 * CHUNK, LANES), f32) for _ in range(2)],
            *[pltpu.VMEM((SZ, 4 * CHUNK, LANES), f32) for _ in range(2)],
            pltpu.VMEM((ROWS, LANES), f32),
            dma((3,)),
            dma((2 * CHUNKS,)),
            dma((2 * CHUNKS,)),
            dma((2 * CHUNKS,)),
            dma((2 * CHUNKS,)),
            dma((2 * CHUNKS,)),
            dma((4,)),
            dma((4,)),
            dma((2 * PLANE,)),
            dma((2 * PLANE,)),
            dma((2 * SZ,)),
            dma((2 * SZ,)),
        ],
        compiler_params=pltpu.CompilerParams(
            collective_id=0, has_side_effects=True, vmem_limit_bytes=24 * 2**20
        ),
    )(flow_state, flow_source, pseudo_step, flux_jacobian, stator_donor, stator_weight, rotor_donor, rotor_weight)


def solution(mesh):
    return jax.shard_map(
        local,
        mesh=mesh,
        in_specs=(
            P("inst", None, "space", None),
            P("inst", None, "space", None),
            P("space", None),
            P(),
            P("inst", "space"),
            P("inst", "space"),
            P("inst", "space"),
            P("inst", "space"),
        ),
        out_specs=(P("inst", None, "space", None), P("inst", None, "space", None)),
        check_vma=False,
    )
```

time: 1460 us -> 60.3 us (0.04)
  the two profiles are of different devices: /device:TPU:2 before, /device:TPU:1 now
where the time goes in v1:
time: 60.3 us; the launch traced here: 60 us
  Pallas kernels  51.2 us (85%)
  local copies, waits for them, and re-layouts  8.08 us (13%)
  between operations  0.66 us (1%)
    pallas_call x1, Pallas kernels, local(): pl.pallas_call(kernel, out_shape=(jax.ShapeDtypeStruct(block, f32), jax.S...  51.2 us
    unnamed x18, local copies, waits for them, and re-layouts  8.08 us

profile of v1, /device:TPU:1, one launch (start us, length us, event | category | flops | bytes accessed | tf_op | source)
XLA Modules:
  0.0 60.0 jit_solution(7860842371595002309)
XLA Ops:
  0.6 0.0 copy-start
  0.6 1.1 %copy-done = f32[2,5,64,256]{3,2,1,0:T(8,128)S(1)} copy-done((f32[2,5,64,256]{3,2,1,0:T(8,128)S(1)}, f32[2,5,64,256]{3,2,1,0:T(8,128)}, u32[]{:S(2)}) %copy-start) | copy-done | bytes 655384
  1.7 0.0 copy-start.1
  1.7 1.1 %copy-done.1 = f32[2,5,64,256]{3,2,1,0:T(8,128)S(1)} copy-done((f32[2,5,64,256]{3,2,1,0:T(8,128)S(1)}, f32[2,5,64,256]{3,2,1,0:T(8,128)}, u32[]{:S(2)}) %copy-start.1) | copy-done | bytes 655384
  2.8 0.0 copy-start.2
  2.8 0.8 %copy-done.2 = f32[64,256]{1,0:T(8,128)S(1)} copy-done((f32[64,256]{1,0:T(8,128)S(1)}, f32[64,256]{1,0:T(8,128)}, u32[]{:S(2)}) %copy-start.2) | copy-done | bytes 65560
  3.6 0.0 copy-start.3
  3.7 0.7 %copy-done.3 = f32[5,5]{1,0:T(8,128)S(1)} copy-done((f32[5,5]{1,0:T(8,128)S(1)}, f32[5,5]{1,0:T(8,128)}, u32[]{:S(2)}) %copy-start.3) | copy-done | bytes 124
  4.3 0.0 copy-start.4
  4.3 0.7 %copy-done.4 = s32[2,64]{1,0:T(2,128)S(1)} copy-done((s32[2,64]{1,0:T(2,128)S(1)}, s32[2,64]{1,0:T(2,128)}, u32[]{:S(2)}) %copy-start.4) | copy-done | bytes 536
  5.0 0.0 copy-start.5
  5.0 0.7 %copy-done.5 = f32[2,64]{1,0:T(2,128)S(1)} copy-done((f32[2,64]{1,0:T(2,128)S(1)}, f32[2,64]{1,0:T(2,128)}, u32[]{:S(2)}) %copy-start.5) | copy-done | bytes 536
  5.7 0.0 copy-start.6
  5.7 0.7 %copy-done.6 = s32[2,64]{1,0:T(2,128)S(1)} copy-done((s32[2,64]{1,0:T(2,128)S(1)}, s32[2,64]{1,0:T(2,128)}, u32[]{:S(2)}) %copy-start.6) | copy-done | bytes 536
  6.4 0.0 copy-start.7
  6.4 0.7 %copy-done.7 = f32[2,64]{1,0:T(2,128)S(1)} copy-done((f32[2,64]{1,0:T(2,128)S(1)}, f32[2,64]{1,0:T(2,128)}, u32[]{:S(2)}) %copy-start.7) | copy-done | bytes 536
  7.1 51.2 %shard_map.95 = (f32[2,5,64,256]{3,2,1,0:T(8,128)S(1)}, f32[2,5,64,256]{3,2,1,0:T(8,128)S(1)}) custom-call(f32[2,5,64,256]{3,2,1,0:T(8,128)S(1)} %copy-done, f32[2,5,64,256]{3,2,1,0:T(8,128)S(1)} %copy-done.1, f32[64,256]{1,0:T(8,128)S(1)} %copy-done.2, f32[5,5]{1,0:T(8,128)S(1)} %copy-done.3, s32[2,64]{1,0:T(2,128)S(1)} %copy-done.4, ...), custom_call_target="tpu_custom_call" | custom-call | tf_op jit(solution)/shard_map/pallas_call | solution.py:361
  58.3 0.8 %copy.12 = f32[2,5,64,256]{3,2,1,0:T(8,128)} copy(f32[2,5,64,256]{3,2,1,0:T(8,128)S(1)} %get-tuple-element.4) | data formatting | bytes 1310720
  59.1 0.8 %copy.13 = f32[2,5,64,256]{3,2,1,0:T(8,128)} copy(f32[2,5,64,256]{3,2,1,0:T(8,128)S(1)} %get-tuple-element.5) | data formatting | bytes 1310720
Async XLA Ops:
  0.6 1.1 %copy-start = (f32[2,5,64,256]{3,2,1,0:T(8,128)S(1)}, f32[2,5,64,256]{3,2,1,0:T(8,128)}, u32[]{:S(2)}) copy-start(f32[2,5,64,256]{3,2,1,0:T(8,128)} %flow_hbm.1) | copy-start | bytes 1966084
  1.7 1.1 %copy-start.1 = (f32[2,5,64,256]{3,2,1,0:T(8,128)S(1)}, f32[2,5,64,256]{3,2,1,0:T(8,128)}, u32[]{:S(2)}) copy-start(f32[2,5,64,256]{3,2,1,0:T(8,128)} %source_hbm.1) | copy-start | bytes 1966084
  2.8 0.8 %copy-start.2 = (f32[64,256]{1,0:T(8,128)S(1)}, f32[64,256]{1,0:T(8,128)}, u32[]{:S(2)}) copy-start(f32[64,256]{1,0:T(8,128)} %step_hbm.1) | copy-start | bytes 196612
  3.6 0.7 %copy-start.3 = (f32[5,5]{1,0:T(8,128)S(1)}, f32[5,5]{1,0:T(8,128)}, u32[]{:S(2)}) copy-start(f32[5,5]{1,0:T(8,128)} %jac.1) | copy-start | bytes 304
  4.3 0.7 %copy-start.4 = (s32[2,64]{1,0:T(2,128)S(1)}, s32[2,64]{1,0:T(2,128)}, u32[]{:S(2)}) copy-start(s32[2,64]{1,0:T(2,128)} %stator_donor.1) | copy-start | bytes 1540
  5.0 0.7 %copy-start.5 = (f32[2,64]{1,0:T(2,128)S(1)}, f32[2,64]{1,0:T(2,128)}, u32[]{:S(2)}) copy-start(f32[2,64]{1,0:T(2,128)} %stator_weight.1) | copy-start | bytes 1540
  5.7 0.7 %copy-start.6 = (s32[2,64]{1,0:T(2,128)S(1)}, s32[2,64]{1,0:T(2,128)}, u32[]{:S(2)}) copy-start(s32[2,64]{1,0:T(2,128)} %rotor_donor.1) | copy-start | bytes 1540
  6.4 0.7 %copy-start.7 = (f32[2,64]{1,0:T(2,128)S(1)}, f32[2,64]{1,0:T(2,128)}, u32[]{:S(2)}) copy-start(f32[2,64]{1,0:T(2,128)} %rotor_weight.1) | copy-start | bytes 1540

commit v2 on v1

--- a/solution.py
+++ b/solution.py
@@ -19,6 +19,7 @@
 SPACE = SX * SZ * SY
 PLANE = SX * SY
 VISCOSITY = 0.5
+AT_PLANES, AT_RINGS, AT_HALOS = 3, 5, 6
 
 
 def spectral(gap):
@@ -29,18 +30,29 @@
 
 
 def kernel(
-    flow_hbm, source_hbm, step_hbm, jac, stator_donor, stator_weight, rotor_donor, rotor_weight,
-    state_hbm, resid_hbm,
-    flow0, flow1, source, step, sib0, sib1, send0, send1, recv0, recv1, out_state, out_resid,
-    corner, plane0, plane1, ring0, ring1, inflow,
-    load_sem, out_sem, sib_ssem, sib_rsem, par_ssem, par_rsem, halo_ssem, halo_rsem,
-    plane_ssem, plane_rsem, ring_ssem, ring_rsem,
+    flow_hbm, source_hbm, step_hbm, *rest,
+):
+    *small_hbm, out_state, out_resid = rest[:7]
+    body(flow_hbm, source_hbm, step_hbm, small_hbm, out_state, out_resid, *rest[7:])
+
+
+def body(
+    flow_hbm, source_hbm, step_hbm, small_hbm, out_state, out_resid,
+    jac, stator_donor, stator_weight, rotor_donor, rotor_weight,
+    flow0, flow1, source, step, sib0, sib1, send0, send1, recv0, recv1,
+    corner, plane0, plane1, ring0, ring1, inflow, columns, remote_part,
+    halo_out0, halo_out1, halo_in0, halo_in1,
+    known, load_sem, sib_ssem, sib_rsem, par_ssem, par_rsem, halo_ssem, halo_rsem,
+    plane_ssem, plane_rsem, ring_ssem, ring_rsem, column_ssem, column_rsem,
 ):
     inst, space = lax.axis_index("inst"), lax.axis_index("space")
     pair, core = inst // 2, inst % 2
     x, z, y = space // (SZ * SY), (space // SY) % SZ, space % SY
     sibling = (pair * 2 + 1 - core, space)
     partner = ((1 - pair) * 2 + core, space)
+    diagonal = ((1 - pair) * 2 + 1 - core, space)
+    across = (inst, (space + SPACE // 2) % SPACE)
+    middle = ((1 - pair) * 2 + core, (space + SPACE // 2) % SPACE)
     above = (inst, (space + SPACE - 1) % SPACE)
     below = (inst, (space + 1) % SPACE)
     slot = x * SY + y
@@ -60,13 +72,41 @@
     flow_in.start()
     source_in.start()
     step_in.start()
-
+    small = (jac, stator_donor, stator_weight, rotor_donor, rotor_weight)
+    small_in = [
+        pltpu.make_async_copy(src, dst, load_sem.at[3 + k]) for k, (src, dst) in enumerate(zip(small_hbm, small))
+    ]
+    for copy in small_in:
+        copy.start()
+
+    def on_line(k, along_y, along_z):
+        out = []
+        if along_y:
+            out += [(y >= k, (inst, space - k)), (y < SY - k, (inst, space + k))]
+        if along_z:
+            out += [(z >= k, (inst, space - k * SY)), (z < SZ - k, (inst, space + k * SY))]
+        return out
+
+    always = space >= 0
+    nearest = [(always, partner), (x != pair, middle)] + on_line(1, True, True)
+
+    def tell(semaphore, devices):
+        for exists, device in devices:
+
+            @pl.when(exists)
+            def _(device=device):
+                pl.semaphore_signal(semaphore, inc=1, device_id=device, device_id_type=MESH)
+
+    def hear(semaphore, devices):
+        count = 0
+        for exists, _ in devices:
+            count = count + exists.astype(jnp.int32)
+        pl.semaphore_wait(semaphore, count)
+
+    rounds = [nearest, on_line(2, True, True), on_line(4, False, True) + [(always, across)]]
     barrier = pltpu.get_barrier_semaphore()
-    greeted = [sibling, partner, above, below]
-    greeted += [plane_peer(k)[1] for k in range(1, PLANE)]
-    greeted += [ring_peer(k)[1] for k in range(1, SZ)]
-    for device in greeted:
-        pl.semaphore_signal(barrier, inc=1, device_id=device, device_id_type=MESH)
+    greeted = [(always, sibling)] + nearest
+    tell(barrier, greeted)
 
     lane = lax.broadcasted_iota(jnp.int32, (CHUNK, LANES), 1)
     low = lane < ROWS
@@ -97,17 +137,38 @@
         at = sweep * CHUNKS + g
         return remote(send.at[g], recv.at[g], par_ssem.at[at], par_rsem.at[at], partner)
 
+    halos_out, halos_in = (halo_out0, halo_out1), (halo_in0, halo_in1)
+
     def halo_copies(sweep):
-        flow = flow0 if sweep == 0 else flow1
-        first = flow.at[:, :, pl.ds(CHUNK, 1), :]
-        last = flow.at[:, :, pl.ds(CHUNK + ROWS - 1, 1), :]
-        before = flow.at[:, :, pl.ds(CHUNK - 1, 1), :]
-        after = flow.at[:, :, pl.ds(CHUNK + ROWS, 1), :]
+        out, into = halos_out[sweep], halos_in[sweep]
         up, down = 2 * sweep, 2 * sweep + 1
         return (
-            remote(first, after, halo_ssem.at[up], halo_rsem.at[up], above),
-            remote(last, before, halo_ssem.at[down], halo_rsem.at[down], below),
+            remote(out.at[0], into.at[1], halo_ssem.at[up], halo_rsem.at[up], above),
+            remote(out.at[1], into.at[0], halo_ssem.at[down], halo_rsem.at[down], below),
         )
+
+    def pack_halos(sweep):
+        flow, out = (flow0 if sweep == 0 else flow1), halos_out[sweep]
+        for side, row in enumerate((CHUNK, CHUNK + ROWS - 1)):
+            for n in range(2):
+                for v in range(NV):
+                    out[side, n, pl.ds(v, 1), :] = flow[n, v, pl.ds(row, 1), :]
+
+    def unpack_halos(sweep):
+        flow, into = (flow0 if sweep == 0 else flow1), halos_in[sweep]
+        for copy in halo_copies(sweep):
+            copy.wait_recv()
+        for side, row in enumerate((CHUNK - 1, CHUNK + ROWS)):
+            for n in range(2):
+                for v in range(NV):
+                    flow[n, v, pl.ds(row, 1), :] = into[side, n, pl.ds(v, 1), :]
+
+    def column_copies():
+        mine = plane1.at[slot]
+        return [
+            remote(mine, columns.at[k], column_ssem.at[k], column_rsem.at[k], device)
+            for k, device in enumerate((sibling, partner, diagonal))
+        ]
 
     def plane_copy(sweep, k):
         _, device = plane_peer(k)
@@ -201,19 +262,21 @@
                         + (to_sib[a][0] * other[0] + to_sib[a][1] * other[1])
                     )
 
-    jacobian = [[jac[v, w] for w in range(NV)] for v in range(NV)]
-
     def advance(sweep, g):
         flow, sib, recv = (flow0, sib0, recv0) if sweep == 0 else (flow1, sib1, recv1)
         here = pl.ds(pl.multiple_of(g * CHUNK, CHUNK), CHUNK)
-        entering = inflow[here, :]
+        jacobian = [[jac[v, w] for w in range(NV)] for v in range(NV)]
+        entering = inflow[here, :] if sweep == 1 else None
         for t in range(2):
             at = pl.ds(t * LANES, LANES)
             pace = step[here, at]
+            edge = lane == (LANES - 1 if t == 0 else 0)
             centre = []
             for n in range(2):
                 centre.append([flow[n, v, rows_at(g), at] for v in range(NV)])
             for n in range(2):
+                if sweep == 1:
+                    fixed = remote_part[pl.ds(pl.multiple_of(n * ROWS + g * CHUNK, CHUNK), CHUNK), :]
                 diff, smooth = [], []
                 for v in range(NV):
                     window = flow[n, v, pl.ds(pl.multiple_of(g * CHUNK, CHUNK), 3 * CHUNK), at]
@@ -221,33 +284,68 @@
                     lower = window[CHUNK + 1 : 2 * CHUNK + 1]
                     f = centre[n][v]
                     left, right = pltpu.roll(f, 1, axis=1), pltpu.roll(f, LANES - 1, axis=1)
-                    q = (1 - t) * 2 * CHUNK + n * CHUNK + v
-                    if t == 0:
-                        q = 2 * CHUNK + n * CHUNK + v
-                        left = jnp.where(lane == 0, 0.0, left)
-                        right = jnp.where(lane == LANES - 1, pltpu.roll(entering, LANES - 1 - q, axis=1), right)
-                    else:
-                        q = n * CHUNK + v
-                        left = jnp.where(lane == 0, pltpu.roll(entering, (LANES - q) % LANES, axis=1), left)
-                        right = jnp.where(lane == LANES - 1, 0.0, right)
+                    enter_left = enter_right = 0.0
+                    if sweep == 1:
+                        if t == 0:
+                            enter_right = pltpu.roll(entering, LANES - 1 - (2 * CHUNK + n * CHUNK + v), axis=1)
+                        else:
+                            enter_left = pltpu.roll(entering, (LANES - n * CHUNK - v) % LANES, axis=1)
+                    left = jnp.where(lane == 0, enter_left, left)
+                    right = jnp.where(lane == LANES - 1, enter_right, right)
                     diff.append(f - left)
                     smooth.append(VISCOSITY * (4.0 * f - left - right - upper - lower))
                 for v in range(NV):
                     convect = jacobian[v][0] * diff[0]
                     for w in range(1, NV):
                         convect = convect + jacobian[v][w] * diff[w]
-                    derivative = (
-                        from_own[n][0] * centre[0][v] + from_own[n][1] * centre[1][v]
-                        + (from_sib[n][0] * sib[g, 0, v, :, at] + from_sib[n][1] * sib[g, 1, v, :, at])
+                    others = (
+                        from_sib[n][0] * sib[g, 0, v, :, at] + from_sib[n][1] * sib[g, 1, v, :, at]
                         + recv[g, n, v, :, at]
                     )
+                    if sweep == 1:
+                        turn = LANES - 1 - v if t == 0 else LANES - CHUNK - v
+                        others = jnp.where(edge, pltpu.roll(fixed, turn, axis=1), others)
+                    derivative = from_own[n][0] * centre[0][v] + from_own[n][1] * centre[1][v] + others
                     residual = convect + smooth[v] + derivative - source[n, v, here, at]
                     new = centre[n][v] - pace * residual
                     if sweep == 0:
                         flow1[n, v, rows_at(g), at] = new
                     else:
-                        out_state[g, n, v, :, at] = new
-                        out_resid[g, n, v, :, at] = residual
+                        out_state[n, v, here, at] = new
+                        out_resid[n, v, here, at] = residual
+
+    def patch(g):
+        here = pl.ds(pl.multiple_of(g * CHUNK, CHUNK), CHUNK)
+        jacobian = [[jac[v, w] for w in range(NV)] for v in range(NV)]
+        entering = inflow[here, :]
+        for n in range(2):
+            at = pl.ds(0, LANES)
+            pace = jnp.where(lane == LANES - 1, step[here, at], 0.0)
+            for v in range(NV):
+                right = pltpu.roll(entering, LANES - 1 - (2 * CHUNK + n * CHUNK + v), axis=1)
+                flow1[n, v, rows_at(g), at] = flow1[n, v, rows_at(g), at] + pace * (VISCOSITY * right)
+            at = pl.ds(LANES, LANES)
+            pace = jnp.where(lane == 0, step[here, at], 0.0)
+            left = [pltpu.roll(entering, (LANES - n * CHUNK - v) % LANES, axis=1) for v in range(NV)]
+            for v in range(NV):
+                share = VISCOSITY * left[v]
+                for w in range(NV):
+                    share = share + jacobian[v][w] * left[w]
+                flow1[n, v, rows_at(g), at] = flow1[n, v, rows_at(g), at] + pace * share
+
+    def mix_columns():
+        total = None
+        for k, table in enumerate((from_sib, to_own, to_sib)):
+            straight = columns[k]
+            turned = pltpu.roll(straight, ROWS, axis=1)
+            low2 = lax.broadcasted_iota(jnp.int32, (2 * CHUNK, LANES), 1) < ROWS
+            same = jnp.where(low2, table[0][0], table[1][1])
+            cross = jnp.where(low2, table[0][1], table[1][0])
+            term = same * straight + cross * turned
+            total = term if total is None else total + term
+        corner[...] = jnp.zeros_like(corner)
+        corner[pl.ds(0, 2 * CHUNK), :] = total
+        remote_part[...] = corner[...].T
 
     def loop(body):
         def wrapped(g, carry):
@@ -256,90 +354,113 @@
 
         lax.fori_loop(0, CHUNKS, wrapped, 0)
 
-    def out_copies(g):
-        here = pl.ds(pl.multiple_of(g * CHUNK, CHUNK), CHUNK)
-        return (
-            pltpu.make_async_copy(out_state.at[g], state_hbm.at[:, :, here, :], out_sem.at[g]),
-            pltpu.make_async_copy(out_resid.at[g], resid_hbm.at[:, :, here, :], out_sem.at[CHUNKS + g]),
-        )
+    def order(p):
+        return (p + 1) % CHUNKS
 
     flow_in.wait()
     extract(0)
-    pl.semaphore_wait(barrier, len(greeted))
-
-    def start_sib(g):
-        sib_copy(0, g).start()
-
-    loop(start_sib)
-    for k in range(1, PLANE):
-        plane_copy(0, k).start()
-    for copy in halo_copies(0):
-        copy.start()
-
-    def first_mix(g):
+    pack_halos(0)
+    hear(barrier, greeted)
+    tell(known.at[0], rounds[0])
+    loop(lambda p: sib_copy(0, order(p)).start())
+
+    def first_mix(p):
+        g = order(p)
         sib_copy(0, g).wait_recv()
         mix(0, g)
         par_copy(0, g).start()
 
     loop(first_mix)
-
-    def interface(sweep):
+    for copy in small_in:
+        copy.wait()
+    source_in.wait()
+    step_in.wait()
+    for k in range(2):
+        hear(known.at[k], rounds[k])
+        tell(known.at[k + 1], rounds[k + 1])
+
+    def start_planes(sweep):
+        for k in range(1, PLANE):
+            plane_copy(sweep, k).start()
+
+    def start_rings(sweep):
         for k in range(1, PLANE):
             plane_arrival(sweep, k).wait_recv()
         forward(sweep)
         for k in range(1, SZ):
             ring_copy(sweep, k).start()
+
+    def finish_rings(sweep):
         for k in range(1, SZ):
             ring_arrival(sweep, k).wait_recv()
         interpolate(sweep)
 
-    interface(0)
-    for copy in halo_copies(0):
-        copy.wait_recv()
-    source_in.wait()
-    step_in.wait()
-
-    def second_mix(g):
+    def second_mix(p):
+        g = order(p)
         sib_copy(1, g).wait_recv()
         mix(1, g)
         par_copy(1, g).start()
 
-    def first_sweep(g):
+    def first_sweep(p):
+        g = order(p)
+
+        @pl.when(p == AT_PLANES)
+        def _():
+            hear(known.at[2], rounds[2])
+            start_planes(0)
+
+        @pl.when(p == AT_RINGS)
+        def _():
+            start_rings(0)
+            for copy in halo_copies(0):
+                copy.start()
+
+        @pl.when(p == AT_HALOS)
+        def _():
+            unpack_halos(0)
+
         par_copy(0, g).wait_recv()
         advance(0, g)
         sib_copy(1, g).start()
 
-        @pl.when(g > 0)
+        @pl.when(p > 0)
         def _():
-            second_mix(g - 1)
+            second_mix(p - 1)
 
     loop(first_sweep)
+    second_mix(CHUNKS - 1)
+    finish_rings(0)
+    loop(lambda p: sib_copy(1, order(p)).wait_send())
+    loop(patch)
+    extract(1)
+    start_planes(1)
+    pack_halos(1)
     for copy in halo_copies(1):
         copy.start()
-    extract(1)
-    for k in range(1, PLANE):
-        plane_copy(1, k).start()
-    second_mix(CHUNKS - 1)
-    interface(1)
-    for copy in halo_copies(1):
+    for copy in column_copies():
+        copy.start()
+    start_rings(1)
+    unpack_halos(1)
+    for copy in column_copies():
         copy.wait_recv()
-
-    def second_sweep(g):
+    mix_columns()
+    finish_rings(1)
+
+    def second_sweep(p):
+        g = order(p)
         par_copy(1, g).wait_recv()
         advance(1, g)
-        for copy in out_copies(g):
-            copy.start()
 
     loop(second_sweep)
 
     def finish(g):
+        sib_copy(0, g).wait_send()
         for sweep in range(2):
-            sib_copy(sweep, g).wait_send()
             par_copy(sweep, g).wait_send()
-        for copy in out_copies(g):
-            copy.wait()
 
     loop(finish)
+    for copy in column_copies():
+        copy.wait_send()
     for sweep in range(2):
         for copy in halo_copies(sweep):
             copy.wait_send()
@@ -349,32 +470,55 @@
             ring_copy(sweep, k).wait_send()
 
 
+def store(state, resid, state_hbm, resid_hbm, sems):
+    copies = [
+        pltpu.make_async_copy(state, state_hbm, sems.at[0]),
+        pltpu.make_async_copy(resid, resid_hbm, sems.at[1]),
+    ]
+    for copy in copies:
+        copy.start()
+    for copy in copies:
+        copy.wait()
+
+
 def local(flow_state, flow_source, pseudo_step, flux_jacobian, stator_donor, stator_weight, rotor_donor, rotor_weight):
     f32 = jnp.float32
     block = (2, NV, ROWS, AX)
     padded = (2, NV, ROWS + 2 * CHUNK, AX)
     chunked = (CHUNKS, 2, NV, CHUNK, AX)
-    anywhere = pl.BlockSpec(memory_space=pl.ANY)
-    smem = pl.BlockSpec(memory_space=pltpu.SMEM)
+    anywhere = pl.BlockSpec(memory_space=pltpu.HBM)
     vmem = pl.BlockSpec(memory_space=pltpu.VMEM)
     dma = pltpu.SemaphoreType.DMA
-    return pl.pallas_call(
+    regular = pltpu.SemaphoreType.REGULAR
+    halo = (2, 2, NV, AX)
+    args = (
+        flow_state, flow_source, pseudo_step, flux_jacobian, stator_donor, stator_weight, rotor_donor, rotor_weight
+    )
+    state, resid = pl.pallas_call(
         kernel,
-        out_shape=(jax.ShapeDtypeStruct(block, f32), jax.ShapeDtypeStruct(block, f32)),
-        in_specs=[anywhere, anywhere, anywhere, smem, smem, vmem, smem, vmem],
-        out_specs=(anywhere, anywhere),
+        out_shape=(pltpu.VMEM(block, f32), pltpu.VMEM(block, f32)),
+        in_specs=[anywhere] * 8,
+        out_specs=(vmem, vmem),
         scratch_shapes=[
+            pltpu.SMEM((NV, NV), f32),
+            pltpu.SMEM((2, ROWS), jnp.int32),
+            pltpu.VMEM((2, ROWS), f32),
+            pltpu.SMEM((2, ROWS), jnp.int32),
+            pltpu.VMEM((2, ROWS), f32),
             pltpu.VMEM(padded, f32),
             pltpu.VMEM(padded, f32),
             pltpu.VMEM(block, f32),
             pltpu.VMEM((ROWS, AX), f32),
-            *[pltpu.VMEM(chunked, f32) for _ in range(8)],
+            *[pltpu.VMEM(chunked, f32) for _ in range(6)],
             pltpu.VMEM((LANES, LANES), f32),
             *[pltpu.VMEM((PLANE, 2 * CHUNK, LANES), f32) for _ in range(2)],
             *[pltpu.VMEM((SZ, 4 * CHUNK, LANES), f32) for _ in range(2)],
             pltpu.VMEM((ROWS, LANES), f32),
-            dma((3,)),
-            dma((2 * CHUNKS,)),
+            pltpu.VMEM((3, 2 * CHUNK, LANES), f32),
+            pltpu.VMEM((LANES, LANES), f32),
+            *[pltpu.VMEM(halo, f32) for _ in range(4)],
+            regular((3,)),
+            dma((8,)),
             dma((2 * CHUNKS,)),
             dma((2 * CHUNKS,)),
             dma((2 * CHUNKS,)),
@@ -385,11 +529,22 @@
             dma((2 * PLANE,)),
             dma((2 * SZ,)),
             dma((2 * SZ,)),
+            dma((3,)),
+            dma((3,)),
         ],
         compiler_params=pltpu.CompilerParams(
             collective_id=0, has_side_effects=True, vmem_limit_bytes=24 * 2**20
         ),
-    )(flow_state, flow_source, pseudo_step, flux_jacobian, stator_donor, stator_weight, rotor_donor, rotor_weight)
+    )(*[pltpu.with_memory_space_constraint(arg, pltpu.HBM) for arg in args])
+    return pl.pallas_call(
+        store,
+        out_shape=(pltpu.HBM(block, f32), pltpu.HBM(block, f32)),
+        in_specs=[vmem, vmem],
+        out_specs=(anywhere, anywhere),
+        scratch_shapes=[dma((2,))],
+    )(
+        pltpu.with_memory_space_constraint(state, pltpu.VMEM), pltpu.with_memory_space_constraint(resid, pltpu.VMEM)
+    )
 
 
 def solution(mesh):

time: 60.3 us -> 57.2 us (0.949)
  the two profiles are of different devices: /device:TPU:1 before, /device:TPU:2 now
where the time goes in v2:
time: 57.2 us; the launch traced here: 57.1 us
  Pallas kernels  56.5 us (99%)
  between operations  0.64 us (1%)
    pallas_call x1, Pallas kernels, local(): pl.pallas_call(kernel, out_shape=(pltpu.VMEM(block, f32), pltpu.VMEM(bloc...  55.4 us

profile of v2, /device:TPU:2, one launch (start us, length us, event | category | flops | bytes accessed | tf_op | source)
XLA Modules:
  0.0 57.1 jit_solution(15372627892052799378)
XLA Ops:
  0.6 55.4 %shard_map.95 = (f32[2,5,64,256]{3,2,1,0:T(8,128)S(1)}, f32[2,5,64,256]{3,2,1,0:T(8,128)S(1)}) custom-call(f32[2,5,64,256]{3,2,1,0:T(8,128)} %flow_hbm.1, f32[2,5,64,256]{3,2,1,0:T(8,128)} %source_hbm.1, f32[64,256]{1,0:T(8,128)} %step_hbm.1, f32[5,5]{1,0:T(8,128)} %rest_0_.1, s32[2,64]{1,0:T(2,128)} %rest_1_.1, f32[2,64]{1,0:T(2,128)} %rest_2_.1, ...), custom_call_target="tpu_custom_call" | custom-call | tf_op jit(solution)/shard_map/pallas_call | solution.py:497
  56.1 1.1 %shard_map.96 = (f32[2,5,64,256]{3,2,1,0:T(8,128)}, f32[2,5,64,256]{3,2,1,0:T(8,128)}) custom-call(f32[2,5,64,256]{3,2,1,0:T(8,128)S(1)} %get-tuple-element.4.state, f32[2,5,64,256]{3,2,1,0:T(8,128)S(1)} %get-tuple-element.5.resid), custom_call_target="tpu_custom_call" | custom-call | tf_op jit(solution)/shard_map/pallas_call | solution.py:539

commit v3 on v2

--- a/solution.py
+++ b/solution.py
@@ -17,9 +17,9 @@
 CHUNKS = ROWS // CHUNK
 SX, SZ, SY = 2, 8, 4
 SPACE = SX * SZ * SY
-PLANE = SX * SY
 VISCOSITY = 0.5
-AT_PLANES, AT_RINGS, AT_HALOS = 3, 5, 6
+AT_RINGS, AT_HALO_SENDS, AT_HALOS = 3, 5, 6
+FIRST = 2
 
 
 def spectral(gap):
@@ -40,10 +40,10 @@
     flow_hbm, source_hbm, step_hbm, small_hbm, out_state, out_resid,
     jac, stator_donor, stator_weight, rotor_donor, rotor_weight,
     flow0, flow1, source, step, sib0, sib1, send0, send1, recv0, recv1,
-    corner, plane0, plane1, ring0, ring1, inflow, columns, remote_part,
+    corner, plane0, plane1, ring0, ring1, cross, inflow, columns, remote_part,
     halo_out0, halo_out1, halo_in0, halo_in1,
     known, load_sem, sib_ssem, sib_rsem, par_ssem, par_rsem, halo_ssem, halo_rsem,
-    plane_ssem, plane_rsem, ring_ssem, ring_rsem, column_ssem, column_rsem,
+    plane_ssem, plane_rsem, ring_ssem, ring_rsem, cross_ssem, cross_rsem, column_ssem, column_rsem,
 ):
     inst, space = lax.axis_index("inst"), lax.axis_index("space")
     pair, core = inst // 2, inst % 2
@@ -55,12 +55,11 @@
     middle = ((1 - pair) * 2 + core, (space + SPACE // 2) % SPACE)
     above = (inst, (space + SPACE - 1) % SPACE)
     below = (inst, (space + 1) % SPACE)
-    slot = x * SY + y
     planes, rings = (plane0, plane1), (ring0, ring1)
 
     def plane_peer(k):
-        other = (slot + k) % PLANE
-        return other, (inst, (other // SY) * (SZ * SY) + z * SY + other % SY)
+        other = (y + k) % SY
+        return other, (inst, x * (SZ * SY) + z * SY + other)
 
     def ring_peer(k):
         other = (z + k) % SZ
@@ -103,13 +102,13 @@
             count = count + exists.astype(jnp.int32)
         pl.semaphore_wait(semaphore, count)
 
-    rounds = [nearest, on_line(2, True, True), on_line(4, False, True) + [(always, across)]]
+    rounds = [nearest, on_line(2, True, True), on_line(4, False, True), on_line(SZ - 1, False, True)]
     barrier = pltpu.get_barrier_semaphore()
     greeted = [(always, sibling)] + nearest
     tell(barrier, greeted)
 
     lane = lax.broadcasted_iota(jnp.int32, (CHUNK, LANES), 1)
-    low = lane < ROWS
+    low = lax.broadcasted_iota(jnp.int32, (NV, LANES), 1) < ROWS
 
     def scalars(table):
         return [[table(a - b) for b in range(2)] for a in range(2)]
@@ -164,7 +163,7 @@
                     flow[n, v, pl.ds(row, 1), :] = into[side, n, pl.ds(v, 1), :]
 
     def column_copies():
-        mine = plane1.at[slot]
+        mine = plane1.at[y]
         return [
             remote(mine, columns.at[k], column_ssem.at[k], column_rsem.at[k], device)
             for k, device in enumerate((sibling, partner, diagonal))
@@ -172,13 +171,21 @@
 
     def plane_copy(sweep, k):
         _, device = plane_peer(k)
-        mine = planes[sweep].at[slot]
-        return remote(mine, mine, plane_ssem.at[sweep * PLANE + k], plane_rsem.at[sweep * PLANE + slot], device)
+        mine = planes[sweep].at[y]
+        return remote(mine, mine, plane_ssem.at[sweep * SY + k], plane_rsem.at[sweep * SY + y], device)
 
     def plane_arrival(sweep, k):
         other, device = plane_peer(k)
         theirs = planes[sweep].at[other]
-        return remote(theirs, theirs, plane_ssem.at[sweep * PLANE + k], plane_rsem.at[sweep * PLANE + other], device)
+        return remote(theirs, theirs, plane_ssem.at[sweep * SY + k], plane_rsem.at[sweep * SY + other], device)
+
+    def cross_copy(sweep):
+        mine = plane0.at[y, x] if sweep == 0 else cross.at[x]
+        return remote(mine, mine, cross_ssem.at[sweep], cross_rsem.at[sweep], across)
+
+    def cross_arrival(sweep):
+        theirs = plane0.at[y, 1 - x] if sweep == 0 else cross.at[1 - x]
+        return remote(theirs, theirs, cross_ssem.at[sweep], cross_rsem.at[sweep], across)
 
     def ring_copy(sweep, k):
         _, device = ring_peer(k)
@@ -206,7 +213,13 @@
             return 0
 
         lax.fori_loop(0, CHUNKS, body, 0)
-        planes[sweep][slot] = corner[...].T[0 : 2 * CHUNK, :]
+        turned = corner[...].T
+        for c in range(2):
+            found = turned[c * CHUNK : c * CHUNK + NV, :]
+            if sweep == 0:
+                plane0[y, x, c] = found
+            else:
+                plane1[y, c] = found
 
     def donor(c, n):
         return (stator_donor if c == 0 else rotor_donor)[n, 0]
@@ -221,32 +234,46 @@
                     carry = (y + dy) // SY
                     wants = (z + 2 * SZ - dz - carry) % SZ
                     over = (wants + dz + carry) // SZ
-                    pick = ((x + dx + over) % SX) * SY + (y + dy) % SY
-                    halves.append(planes[sweep][pick, pl.ds(c * CHUNK, CHUNK), :])
+                    if sweep == 0:
+                        halves.append(plane0[(y + dy) % SY, (x + dx + over) % SX, c])
+                    else:
+                        halves.append(plane1[(y + dy) % SY, c])
                 first, second = halves
                 if n == 0:
                     both = jnp.where(low, first, pltpu.roll(second, ROWS, axis=1))
                 else:
                     both = jnp.where(low, pltpu.roll(first, ROWS, axis=1), second)
-                rings[sweep][z, pl.ds((c * 2 + n) * CHUNK, CHUNK), :] = both
+                rings[sweep][z, c * 2 + n] = both
+
+    def from_ring(sweep, c, n):
+        block = donor(c, n) // ROWS
+        here = rings[sweep][(block // SY) % SZ, c * 2 + n]
+        there = rings[sweep][((block + 1) // SY) % SZ, c * 2 + n]
+        return jnp.where(low, here, there)
+
+    def pass_across():
+        for c in range(2):
+            for n in range(2):
+                cross[x, c * 2 + n] = from_ring(1, c, n)
+
+    def from_cross(c, n):
+        block = donor(c, n) // ROWS
+        here = cross[(block // (SZ * SY)) % SX, c * 2 + n]
+        there = cross[((block + 1) // (SZ * SY)) % SX, c * 2 + n]
+        return jnp.where(low, here, there)
 
     def interpolate(sweep):
         corner[...] = jnp.zeros_like(corner)
         for c in range(2):
             weights = stator_weight if c == 0 else rotor_weight
             for n in range(2):
-                start = donor(c, n)
-                block = start // ROWS
-                group = pl.ds((c * 2 + n) * CHUNK, CHUNK)
-                here = rings[sweep][(block // SY) % SZ, group, :]
-                there = rings[sweep][((block + 1) // SY) % SZ, group, :]
-                window = jnp.where(low, here, there)
-                offset = start % ROWS
+                window = from_ring(sweep, c, n) if sweep == 0 else from_cross(c, n)
+                offset = donor(c, n) % ROWS
                 first = pltpu.roll(window, (LANES - offset) % LANES, axis=1)
                 second = pltpu.roll(window, LANES - 1 - offset, axis=1)
                 weight = weights[pl.ds(n, 1), :]
                 weight = jnp.concatenate([weight, weight], axis=1)
-                corner[group, :] = (1.0 - weight) * first + weight * second
+                corner[pl.ds((c * 2 + n) * CHUNK, NV), :] = (1.0 - weight) * first + weight * second
         inflow[...] = corner[...].T[0:ROWS, :]
 
     def mix(sweep, g):
@@ -266,7 +293,6 @@
         flow, sib, recv = (flow0, sib0, recv0) if sweep == 0 else (flow1, sib1, recv1)
         here = pl.ds(pl.multiple_of(g * CHUNK, CHUNK), CHUNK)
         jacobian = [[jac[v, w] for w in range(NV)] for v in range(NV)]
-        entering = inflow[here, :] if sweep == 1 else None
         for t in range(2):
             at = pl.ds(t * LANES, LANES)
             pace = step[here, at]
@@ -275,23 +301,14 @@
             for n in range(2):
                 centre.append([flow[n, v, rows_at(g), at] for v in range(NV)])
             for n in range(2):
-                if sweep == 1:
-                    fixed = remote_part[pl.ds(pl.multiple_of(n * ROWS + g * CHUNK, CHUNK), CHUNK), :]
                 diff, smooth = [], []
                 for v in range(NV):
                     window = flow[n, v, pl.ds(pl.multiple_of(g * CHUNK, CHUNK), 3 * CHUNK), at]
                     upper = window[CHUNK - 1 : 2 * CHUNK - 1]
                     lower = window[CHUNK + 1 : 2 * CHUNK + 1]
                     f = centre[n][v]
-                    left, right = pltpu.roll(f, 1, axis=1), pltpu.roll(f, LANES - 1, axis=1)
-                    enter_left = enter_right = 0.0
-                    if sweep == 1:
-                        if t == 0:
-                            enter_right = pltpu.roll(entering, LANES - 1 - (2 * CHUNK + n * CHUNK + v), axis=1)
-                        else:
-                            enter_left = pltpu.roll(entering, (LANES - n * CHUNK - v) % LANES, axis=1)
-                    left = jnp.where(lane == 0, enter_left, left)
-                    right = jnp.where(lane == LANES - 1, enter_right, right)
+                    left = jnp.where(lane == 0, 0.0, pltpu.roll(f, 1, axis=1))
+                    right = jnp.where(lane == LANES - 1, 0.0, pltpu.roll(f, LANES - 1, axis=1))
                     diff.append(f - left)
                     smooth.append(VISCOSITY * (4.0 * f - left - right - upper - lower))
                 for v in range(NV):
@@ -303,8 +320,7 @@
                         + recv[g, n, v, :, at]
                     )
                     if sweep == 1:
-                        turn = LANES - 1 - v if t == 0 else LANES - CHUNK - v
-                        others = jnp.where(edge, pltpu.roll(fixed, turn, axis=1), others)
+                        others = jnp.where(edge, 0.0, others)
                     derivative = from_own[n][0] * centre[0][v] + from_own[n][1] * centre[1][v] + others
                     residual = convect + smooth[v] + derivative - source[n, v, here, at]
                     new = centre[n][v] - pace * residual
@@ -314,45 +330,55 @@
                         out_state[n, v, here, at] = new
                         out_resid[n, v, here, at] = residual
 
-    def patch(g):
+    def patch(sweep, g):
         here = pl.ds(pl.multiple_of(g * CHUNK, CHUNK), CHUNK)
         jacobian = [[jac[v, w] for w in range(NV)] for v in range(NV)]
         entering = inflow[here, :]
         for n in range(2):
-            at = pl.ds(0, LANES)
-            pace = jnp.where(lane == LANES - 1, step[here, at], 0.0)
-            for v in range(NV):
-                right = pltpu.roll(entering, LANES - 1 - (2 * CHUNK + n * CHUNK + v), axis=1)
-                flow1[n, v, rows_at(g), at] = flow1[n, v, rows_at(g), at] + pace * (VISCOSITY * right)
-            at = pl.ds(LANES, LANES)
-            pace = jnp.where(lane == 0, step[here, at], 0.0)
+            if sweep == 1:
+                fixed = remote_part[pl.ds(pl.multiple_of(n * ROWS + g * CHUNK, CHUNK), CHUNK), :]
             left = [pltpu.roll(entering, (LANES - n * CHUNK - v) % LANES, axis=1) for v in range(NV)]
-            for v in range(NV):
-                share = VISCOSITY * left[v]
-                for w in range(NV):
-                    share = share + jacobian[v][w] * left[w]
-                flow1[n, v, rows_at(g), at] = flow1[n, v, rows_at(g), at] + pace * share
+            right = [pltpu.roll(entering, LANES - 1 - (2 * CHUNK + n * CHUNK + v), axis=1) for v in range(NV)]
+            for t in range(2):
+                at = pl.ds(t * LANES, LANES)
+                edge = lane == (LANES - 1 if t == 0 else 0)
+                pace = step[here, at]
+                for v in range(NV):
+                    if t == 0:
+                        share = -VISCOSITY * right[v]
+                    else:
+                        share = -VISCOSITY * left[v]
+                        for w in range(NV):
+                            share = share - jacobian[v][w] * left[w]
+                    if sweep == 0:
+                        share = jnp.where(edge, share, 0.0)
+                        flow1[n, v, rows_at(g), at] = flow1[n, v, rows_at(g), at] - pace * share
+                    else:
+                        turn = LANES - 1 - v if t == 0 else LANES - CHUNK - v
+                        share = jnp.where(edge, share + pltpu.roll(fixed, turn, axis=1), 0.0)
+                        out_state[n, v, here, at] = out_state[n, v, here, at] - pace * share
+                        out_resid[n, v, here, at] = out_resid[n, v, here, at] + share
 
     def mix_columns():
-        total = None
-        for k, table in enumerate((from_sib, to_own, to_sib)):
-            straight = columns[k]
-            turned = pltpu.roll(straight, ROWS, axis=1)
-            low2 = lax.broadcasted_iota(jnp.int32, (2 * CHUNK, LANES), 1) < ROWS
-            same = jnp.where(low2, table[0][0], table[1][1])
-            cross = jnp.where(low2, table[0][1], table[1][0])
-            term = same * straight + cross * turned
-            total = term if total is None else total + term
         corner[...] = jnp.zeros_like(corner)
-        corner[pl.ds(0, 2 * CHUNK), :] = total
+        for c in range(2):
+            total = None
+            for k, table in enumerate((from_sib, to_own, to_sib)):
+                straight = columns[k, c]
+                turned = pltpu.roll(straight, ROWS, axis=1)
+                same = jnp.where(low, table[0][0], table[1][1])
+                crossed = jnp.where(low, table[0][1], table[1][0])
+                term = same * straight + crossed * turned
+                total = term if total is None else total + term
+            corner[pl.ds(c * CHUNK, NV), :] = total
         remote_part[...] = corner[...].T
 
-    def loop(body):
+    def loop(body, begin=0, end=CHUNKS):
         def wrapped(g, carry):
             body(g)
             return carry
 
-        lax.fori_loop(0, CHUNKS, wrapped, 0)
+        lax.fori_loop(begin, end, wrapped, 0)
 
     def order(p):
         return (p + 1) % CHUNKS
@@ -370,21 +396,25 @@
         mix(0, g)
         par_copy(0, g).start()
 
-    loop(first_mix)
+    loop(first_mix, 0, FIRST)
+    hear(known.at[0], rounds[0])
+    cross_copy(0).start()
+    tell(known.at[1], rounds[1])
+    loop(first_mix, FIRST, CHUNKS)
     for copy in small_in:
         copy.wait()
     source_in.wait()
     step_in.wait()
-    for k in range(2):
-        hear(known.at[k], rounds[k])
-        tell(known.at[k + 1], rounds[k + 1])
+    hear(known.at[1], rounds[1])
+    tell(known.at[2], rounds[2])
+    cross_arrival(0).wait_recv()
 
     def start_planes(sweep):
-        for k in range(1, PLANE):
+        for k in range(1, SY):
             plane_copy(sweep, k).start()
 
     def start_rings(sweep):
-        for k in range(1, PLANE):
+        for k in range(1, SY):
             plane_arrival(sweep, k).wait_recv()
         forward(sweep)
         for k in range(1, SZ):
@@ -393,7 +423,8 @@
     def finish_rings(sweep):
         for k in range(1, SZ):
             ring_arrival(sweep, k).wait_recv()
-        interpolate(sweep)
+
+    start_planes(0)
 
     def second_mix(p):
         g = order(p)
@@ -404,14 +435,20 @@
     def first_sweep(p):
         g = order(p)
 
-        @pl.when(p == AT_PLANES)
+        @pl.when(p == AT_RINGS)
         def _():
             hear(known.at[2], rounds[2])
-            start_planes(0)
-
-        @pl.when(p == AT_RINGS)
+            start_rings(0)
+            tell(known.at[3], rounds[3])
+
+        @pl.when(p == AT_HALO_SENDS)
         def _():
-            start_rings(0)
+            for exists, _ in rounds[3]:
+
+                @pl.when(exists)
+                def _():
+                    pl.semaphore_wait(known.at[3], 1)
+
             for copy in halo_copies(0):
                 copy.start()
 
@@ -430,8 +467,9 @@
     loop(first_sweep)
     second_mix(CHUNKS - 1)
     finish_rings(0)
+    interpolate(0)
     loop(lambda p: sib_copy(1, order(p)).wait_send())
-    loop(patch)
+    loop(lambda g: patch(0, g))
     extract(1)
     start_planes(1)
     pack_halos(1)
@@ -441,10 +479,9 @@
         copy.start()
     start_rings(1)
     unpack_halos(1)
-    for copy in column_copies():
-        copy.wait_recv()
-    mix_columns()
     finish_rings(1)
+    pass_across()
+    cross_copy(1).start()
 
     def second_sweep(p):
         g = order(p)
@@ -452,6 +489,12 @@
         advance(1, g)
 
     loop(second_sweep)
+    for copy in column_copies():
+        copy.wait_recv()
+    mix_columns()
+    cross_arrival(1).wait_recv()
+    interpolate(1)
+    loop(lambda g: patch(1, g))
 
     def finish(g):
         sib_copy(0, g).wait_send()
@@ -462,9 +505,10 @@
     for copy in column_copies():
         copy.wait_send()
     for sweep in range(2):
+        cross_copy(sweep).wait_send()
         for copy in halo_copies(sweep):
             copy.wait_send()
-        for k in range(1, PLANE):
+        for k in range(1, SY):
             plane_copy(sweep, k).wait_send()
         for k in range(1, SZ):
             ring_copy(sweep, k).wait_send()
@@ -511,13 +555,15 @@
             pltpu.VMEM((ROWS, AX), f32),
             *[pltpu.VMEM(chunked, f32) for _ in range(6)],
             pltpu.VMEM((LANES, LANES), f32),
-            *[pltpu.VMEM((PLANE, 2 * CHUNK, LANES), f32) for _ in range(2)],
-            *[pltpu.VMEM((SZ, 4 * CHUNK, LANES), f32) for _ in range(2)],
+            pltpu.VMEM((SY, SX, 2, NV, LANES), f32),
+            pltpu.VMEM((SY, 2, NV, LANES), f32),
+            *[pltpu.VMEM((SZ, 4, NV, LANES), f32) for _ in range(2)],
+            pltpu.VMEM((SX, 4, NV, LANES), f32),
             pltpu.VMEM((ROWS, LANES), f32),
-            pltpu.VMEM((3, 2 * CHUNK, LANES), f32),
+            pltpu.VMEM((3, 2, NV, LANES), f32),
             pltpu.VMEM((LANES, LANES), f32),
             *[pltpu.VMEM(halo, f32) for _ in range(4)],
-            regular((3,)),
+            regular((4,)),
             dma((8,)),
             dma((2 * CHUNKS,)),
             dma((2 * CHUNKS,)),
@@ -525,10 +571,12 @@
             dma((2 * CHUNKS,)),
             dma((4,)),
             dma((4,)),
-            dma((2 * PLANE,)),
-            dma((2 * PLANE,)),
+            dma((2 * SY,)),
+            dma((2 * SY,)),
             dma((2 * SZ,)),
             dma((2 * SZ,)),
+            dma((2,)),
+            dma((2,)),
             dma((3,)),
             dma((3,)),
         ],

time: 57.2 us -> 44.7 us (0.78)
  the two profiles are of different devices: /device:TPU:2 before, /device:TPU:1 now
where the time goes in v3:
time: 44.7 us; the launch traced here: 44.3 us
  Pallas kernels  43.6 us (98%)
  between operations  0.64 us (1%)
    pallas_call x1, Pallas kernels, local(): pl.pallas_call(kernel, out_shape=(pltpu.VMEM(block, f32), pltpu.VMEM(bloc...  42.6 us
    pallas_call x1, Pallas kernels, local(): pl.pallas_call(store, out_shape=(pltpu.HBM(block, f32), pltpu.HBM(block,...  1.07 us

profile of v3, /device:TPU:1, one launch (start us, length us, event | category | flops | bytes accessed | tf_op | source)
XLA Modules:
  0.0 44.3 jit_solution(11001061031026850453)
XLA Ops:
  0.6 42.6 %shard_map.95 = (f32[2,5,64,256]{3,2,1,0:T(8,128)S(1)}, f32[2,5,64,256]{3,2,1,0:T(8,128)S(1)}) custom-call(f32[2,5,64,256]{3,2,1,0:T(8,128)} %flow_hbm.1, f32[2,5,64,256]{3,2,1,0:T(8,128)} %source_hbm.1, f32[64,256]{1,0:T(8,128)} %step_hbm.1, f32[5,5]{1,0:T(8,128)} %rest_0_.1, s32[2,64]{1,0:T(2,128)} %rest_1_.1, f32[2,64]{1,0:T(2,128)} %rest_2_.1, ...), custom_call_target="tpu_custom_call" | custom-call | tf_op jit(solution)/shard_map/pallas_call | solution.py:541
  43.2 1.1 %shard_map.96 = (f32[2,5,64,256]{3,2,1,0:T(8,128)}, f32[2,5,64,256]{3,2,1,0:T(8,128)}) custom-call(f32[2,5,64,256]{3,2,1,0:T(8,128)S(1)} %get-tuple-element.4.state, f32[2,5,64,256]{3,2,1,0:T(8,128)S(1)} %get-tuple-element.5.resid), custom_call_target="tpu_custom_call" | custom-call | tf_op jit(solution)/shard_map/pallas_call | solution.py:587

commit v4 on v3

v4 whole, which is shorter than its diff:
```python
import math

import jax
import jax.numpy as jnp
from jax import lax
from jax.experimental import pallas as pl
from jax.experimental.pallas import tpu as pltpu
from jax.sharding import PartitionSpec as P

MESH = pl.DeviceIdType.MESH
NT = 8
NV = 5
ROWS = 64
AX = 256
LANES = 128
CHUNK = 8
CHUNKS = ROWS // CHUNK
SX, SZ, SY = 2, 8, 4
SPACE = SX * SZ * SY
LAYER = SZ * SY
VISCOSITY = 0.5
AT_RINGS, AT_HALO_SENDS, AT_HALOS = 3, 5, 6
FIRST = 2


def spectral(gap):
    gap = gap % NT
    if gap == 0:
        return 0.0
    return 0.5 * (-1.0) ** gap * math.cos(math.pi * gap / NT) / math.sin(math.pi * gap / NT)


def kernel(
    flow_hbm, source_hbm, step_hbm, *rest,
):
    *small_hbm, out_state, out_resid = rest[:7]
    body(flow_hbm, source_hbm, step_hbm, small_hbm, out_state, out_resid, *rest[7:])


def body(
    flow_hbm, source_hbm, step_hbm, small_hbm, out_state, out_resid,
    jac, stator_donor, stator_weight, rotor_donor, rotor_weight,
    flow0, flow1, source, step, sib0, sib1, send0, send1, recv0, recv1,
    corner, plane0, plane1, ring0, cross, columns, before, pace_lanes, share_lanes, share_rows,
    halo_out0, halo_out1, halo_in0, halo_in1,
    known, load_sem, sib_ssem, sib_rsem, par_ssem, par_rsem, halo_ssem, halo_rsem,
    plane_ssem, plane_rsem, ring_ssem, ring_rsem, layer_ssem, layer_rsem, cross_ssem, cross_rsem, column_ssem, column_rsem,
):
    inst, space = lax.axis_index("inst"), lax.axis_index("space")
    pair, core = inst // 2, inst % 2
    x, z, y = space // (SZ * SY), (space // SY) % SZ, space % SY
    sibling = (pair * 2 + 1 - core, space)
    partner = ((1 - pair) * 2 + core, space)
    diagonal = ((1 - pair) * 2 + 1 - core, space)
    across = (inst, (space + SPACE // 2) % SPACE)
    above = (inst, (space + SPACE - 1) % SPACE)
    below = (inst, (space + 1) % SPACE)
    place = space % LAYER

    def plane_peer(k):
        return inst, x * LAYER + z * SY + (y + k) % SY

    def ring_peer(k):
        return inst, x * LAYER + ((z + k) % SZ) * SY + y

    def layer_peer(k):
        return inst, x * LAYER + (place + k) % LAYER

    flow_in = pltpu.make_async_copy(flow_hbm, flow0.at[:, :, pl.ds(CHUNK, ROWS), :], load_sem.at[0])
    source_in = pltpu.make_async_copy(source_hbm, source, load_sem.at[1])
    step_in = pltpu.make_async_copy(step_hbm, step, load_sem.at[2])
    flow_in.start()
    source_in.start()
    step_in.start()
    small = (jac, stator_donor, stator_weight, rotor_donor, rotor_weight)
    small_in = [
        pltpu.make_async_copy(src, dst, load_sem.at[3 + k]) for k, (src, dst) in enumerate(zip(small_hbm, small))
    ]
    for copy in small_in:
        copy.start()

    def on_line(k):
        return [(z >= k, (inst, space - k * SY)), (z < SZ - k, (inst, space + k * SY))]

    always = space >= 0
    nearest = [(always, sibling), (always, partner), (always, across)]
    nearest += [(always, plane_peer(k)) for k in range(1, SY)] + on_line(1)

    def tell(semaphore, devices):
        for exists, device in devices:

            @pl.when(exists)
            def _(device=device):
                pl.semaphore_signal(semaphore, inc=1, device_id=device, device_id_type=MESH)

    def hear(semaphore, devices):
        count = 0
        for exists, _ in devices:
            count = count + exists.astype(jnp.int32)
        pl.semaphore_wait(semaphore, count)

    rounds = [on_line(1), on_line(2), on_line(4), on_line(SZ - 1)]
    barrier = pltpu.get_barrier_semaphore()
    tell(barrier, nearest)

    lane = lax.broadcasted_iota(jnp.int32, (CHUNK, LANES), 1)
    low = lax.broadcasted_iota(jnp.int32, (NV, LANES), 1) < ROWS

    def scalars(table):
        return [[table(a - b) for b in range(2)] for a in range(2)]

    from_own = scalars(spectral)
    from_sib = scalars(lambda g: jnp.where(core == 0, spectral(g - 2), spectral(g + 2)).astype(jnp.float32))
    to_own = scalars(lambda g: spectral(g + 4))
    to_sib = scalars(lambda g: jnp.where(core == 0, spectral(g + 2), spectral(g + 6)).astype(jnp.float32))

    def remote(src, dst, ssem, rsem, device):
        return pltpu.make_async_remote_copy(
            src_ref=src, dst_ref=dst, send_sem=ssem, recv_sem=rsem, device_id=device, device_id_type=MESH
        )

    def rows_at(g):
        return pl.ds(pl.multiple_of(CHUNK + g * CHUNK, CHUNK), CHUNK)

    def all_done(ref, semaphore):
        pltpu.make_async_copy(ref, ref, semaphore).wait()

    def sib_copy(sweep, g):
        flow, sib = (flow0, sib0) if sweep == 0 else (flow1, sib1)
        at = sweep * CHUNKS + g
        return remote(flow.at[:, :, rows_at(g), :], sib.at[g], sib_ssem.at[sweep], sib_rsem.at[at], sibling)

    def par_copy(sweep, g):
        send, recv = (send0, recv0) if sweep == 0 else (send1, recv1)
        at = sweep * CHUNKS + g
        return remote(send.at[g], recv.at[g], par_ssem.at[sweep], par_rsem.at[at], partner)

    halos_out, halos_in = (halo_out0, halo_out1), (halo_in0, halo_in1)

    def start_halos(sweep):
        out, into = halos_out[sweep], halos_in[sweep]
        remote(out.at[0], into.at[1], halo_ssem.at[sweep], halo_rsem.at[sweep], above).start()
        remote(out.at[1], into.at[0], halo_ssem.at[sweep], halo_rsem.at[sweep], below).start()

    def pack_halos(sweep):
        flow, out = (flow0 if sweep == 0 else flow1), halos_out[sweep]
        for side, row in enumerate((CHUNK, CHUNK + ROWS - 1)):
            for n in range(2):
                for v in range(NV):
                    out[side, n, pl.ds(v, 1), :] = flow[n, v, pl.ds(row, 1), :]

    def unpack_halos(sweep):
        flow, into = (flow0 if sweep == 0 else flow1), halos_in[sweep]
        all_done(into, halo_rsem.at[sweep])
        for side, row in enumerate((CHUNK - 1, CHUNK + ROWS)):
            for n in range(2):
                for v in range(NV):
                    flow[n, v, pl.ds(row, 1), :] = into[side, n, pl.ds(v, 1), :]

    def cross_copy(sweep):
        mine = plane0.at[y, x] if sweep == 0 else cross.at[x]
        return remote(mine, mine, cross_ssem.at[sweep], cross_rsem.at[sweep], across)

    def cross_arrival(sweep):
        theirs = plane0.at[y, 1 - x] if sweep == 0 else cross.at[1 - x]
        return remote(theirs, theirs, cross_ssem.at[sweep], cross_rsem.at[sweep], across)

    def start_planes():
        mine = plane0.at[y]
        for k in range(1, SY):
            remote(mine, mine, plane_ssem.at[0], plane_rsem.at[0], plane_peer(k)).start()

    def start_rings():
        mine = ring0.at[z]
        for k in range(1, SZ):
            remote(mine, mine, ring_ssem.at[0], ring_rsem.at[0], ring_peer(k)).start()

    def start_layer():
        mine = plane1.at[place]

        def start(k, carry):
            remote(mine, mine, layer_ssem.at[0], layer_rsem.at[0], layer_peer(k)).start()
            return carry

        lax.fori_loop(1, LAYER, start, 0)

    def start_columns():
        mine = plane1.at[place]
        for k, device in enumerate((sibling, partner, diagonal)):
            remote(mine, columns.at[k], column_ssem.at[0], column_rsem.at[0], device).start()

    def gather(sweep, g):
        flow = flow0 if sweep == 0 else flow1
        here = pl.ds(pl.multiple_of(g * CHUNK, CHUNK), CHUNK)
        for n in range(2):
            total = jnp.zeros((CHUNK, LANES), jnp.float32)
            for c in range(2):
                at = pl.ds(c * LANES, LANES)
                tiles = [flow[n, v, rows_at(g), at] for v in range(NV)]
                if sweep == 0:
                    tiles.append(step[here, at])
                for v, tile in enumerate(tiles):
                    q = c * CHUNK + v
                    total = jnp.where(lane == q, pltpu.roll(tile, (q + 1) if c == 0 else q, axis=1), total)
            corner[pl.ds(pl.multiple_of(n * ROWS + g * CHUNK, CHUNK), CHUNK), :] = total

    def turn(sweep):
        turned = corner[...].T
        for c in range(2):
            found = turned[c * CHUNK : c * CHUNK + NV, :]
            if sweep == 0:
                plane0[y, x, c] = found
                pace_lanes[c] = turned[c * CHUNK + NV : c * CHUNK + NV + 1, :]
            else:
                before[c] = found

    def donor(c, n):
        return (stator_donor if c == 0 else rotor_donor)[n, 0]

    def halves(first, second, n):
        if n == 0:
            return jnp.where(low, first, pltpu.roll(second, ROWS, axis=1))
        return jnp.where(low, pltpu.roll(first, ROWS, axis=1), second)

    def forward():
        for c in range(2):
            for n in range(2):
                ahead = (donor(c, n) // ROWS + SPACE - space) % SPACE
                found = []
                for d in (ahead, (ahead + 1) % SPACE):
                    dx, dz, dy = d // LAYER, (d // SY) % SZ, d % SY
                    carry = (y + dy) // SY
                    wants = (z + 2 * SZ - dz - carry) % SZ
                    over = (wants + dz + carry) // SZ
                    found.append(plane0[(y + dy) % SY, (x + dx + over) % SX, c])
                ring0[z, c * 2 + n] = halves(*found, n)

    def from_ring(c, n):
        block = donor(c, n) // ROWS
        here = ring0[(block // SY) % SZ, c * 2 + n]
        there = ring0[((block + 1) // SY) % SZ, c * 2 + n]
        return jnp.where(low, here, there)

    def pass_across():
        for c in range(2):
            for n in range(2):
                block = donor(c, n) // ROWS
                cross[x, c * 2 + n] = halves(plane1[block % LAYER, c], plane1[(block + 1) % LAYER, c], n)

    def from_cross(c, n):
        block = donor(c, n) // ROWS
        here = cross[(block // LAYER) % SX, c * 2 + n]
        there = cross[((block + 1) // LAYER) % SX, c * 2 + n]
        return jnp.where(low, here, there)

    def settle(sweep):
        entering = []
        for c in range(2):
            weights = stator_weight if c == 0 else rotor_weight
            values = []
            for n in range(2):
                window = from_ring(c, n) if sweep == 0 else from_cross(c, n)
                offset = donor(c, n) % ROWS
                first = pltpu.roll(window, (LANES - offset) % LANES, axis=1)
                second = pltpu.roll(window, LANES - 1 - offset, axis=1)
                weight = weights[pl.ds(n, 1), :]
                weight = jnp.concatenate([weight, weight], axis=1)
                values.append((1.0 - weight) * first + weight * second)
            entering.append(jnp.where(low, values[0], pltpu.roll(values[1], ROWS, axis=1)))
        stator, rotor = entering
        share_lanes[0] = -VISCOSITY * rotor
        share_lanes[1] = -VISCOSITY * stator
        for v in range(NV):
            total = share_lanes[1, pl.ds(v, 1), :]
            for w in range(NV):
                total = total - jac[v, w] * stator[w : w + 1, :]
            share_lanes[1, pl.ds(v, 1), :] = total
        if sweep == 1:
            for c in range(2):
                total = share_lanes[c]
                for k, table in enumerate((from_sib, to_own, to_sib)):
                    straight = columns[k, c]
                    turned = pltpu.roll(straight, ROWS, axis=1)
                    same = jnp.where(low, table[0][0], table[1][1])
                    crossed = jnp.where(low, table[0][1], table[1][0])
                    total = total + (same * straight + crossed * turned)
                share_lanes[c] = total

    def turn_share():
        corner[...] = jnp.zeros_like(corner)
        for t in range(2):
            corner[pl.ds(t * CHUNK, NV), :] = share_lanes[t]
        share_rows[...] = corner[...].T

    def mix(sweep, g):
        flow, sib, send = (flow0, sib0, send0) if sweep == 0 else (flow1, sib1, send1)
        for v in range(NV):
            for t in range(2):
                at = pl.ds(t * LANES, LANES)
                own = [flow[n, v, rows_at(g), at] for n in range(2)]
                other = [sib[g, n, v, :, at] for n in range(2)]
                for a in range(2):
                    send[g, a, v, :, at] = (
                        to_own[a][0] * own[0] + to_own[a][1] * own[1]
                        + (to_sib[a][0] * other[0] + to_sib[a][1] * other[1])
                    )

    def advance(sweep, g):
        flow, sib, recv = (flow0, sib0, recv0) if sweep == 0 else (flow1, sib1, recv1)
        here = pl.ds(pl.multiple_of(g * CHUNK, CHUNK), CHUNK)
        jacobian = [[jac[v, w] for w in range(NV)] for v in range(NV)]
        for t in range(2):
            at = pl.ds(t * LANES, LANES)
            pace = step[here, at]
            edge = lane == (LANES - 1 if t == 0 else 0)
            centre = []
            for n in range(2):
                centre.append([flow[n, v, rows_at(g), at] for v in range(NV)])
            for n in range(2):
                diff, smooth = [], []
                for v in range(NV):
                    window = flow[n, v, pl.ds(pl.multiple_of(g * CHUNK, CHUNK), 3 * CHUNK), at]
                    upper = window[CHUNK - 1 : 2 * CHUNK - 1]
                    lower = window[CHUNK + 1 : 2 * CHUNK + 1]
                    f = centre[n][v]
                    left = jnp.where(lane == 0, 0.0, pltpu.roll(f, 1, axis=1))
                    right = jnp.where(lane == LANES - 1, 0.0, pltpu.roll(f, LANES - 1, axis=1))
                    diff.append(f - left)
                    smooth.append(VISCOSITY * (4.0 * f - left - right - upper - lower))
                for v in range(NV):
                    convect = jacobian[v][0] * diff[0]
                    for w in range(1, NV):
                        convect = convect + jacobian[v][w] * diff[w]
                    others = (
                        from_sib[n][0] * sib[g, 0, v, :, at] + from_sib[n][1] * sib[g, 1, v, :, at]
                        + recv[g, n, v, :, at]
                    )
                    if sweep == 1:
                        others = jnp.where(edge, 0.0, others)
                    derivative = from_own[n][0] * centre[0][v] + from_own[n][1] * centre[1][v] + others
                    residual = convect + smooth[v] + derivative - source[n, v, here, at]
                    new = centre[n][v] - pace * residual
                    if sweep == 0:
                        flow1[n, v, rows_at(g), at] = new
                    else:
                        out_state[n, v, here, at] = new
                        out_resid[n, v, here, at] = residual

    def patch(sweep, g):
        here = pl.ds(pl.multiple_of(g * CHUNK, CHUNK), CHUNK)
        for n in range(2):
            shares = share_rows[pl.ds(pl.multiple_of(n * ROWS + g * CHUNK, CHUNK), CHUNK), :]
            for t in range(2):
                at = pl.ds(t * LANES, LANES)
                edge = lane == (LANES - 1 if t == 0 else 0)
                pace = step[here, at]
                for v in range(NV):
                    share = jnp.where(edge, pltpu.roll(shares, LANES - 1 - v if t == 0 else LANES - CHUNK - v, axis=1), 0.0)
                    if sweep == 0:
                        flow1[n, v, rows_at(g), at] = flow1[n, v, rows_at(g), at] - pace * share
                    else:
                        out_state[n, v, here, at] = out_state[n, v, here, at] - pace * share
                        out_resid[n, v, here, at] = out_resid[n, v, here, at] + share

    def loop(body, begin=0, end=CHUNKS):
        def wrapped(g, carry):
            body(g)
            return carry

        lax.fori_loop(begin, end, wrapped, 0)

    def order(p):
        return (p + 1) % CHUNKS

    step_in.wait()
    flow_in.wait()
    loop(lambda g: gather(0, g))
    turn(0)
    pack_halos(0)
    hear(barrier, nearest)
    cross_copy(0).start()
    tell(known.at[0], rounds[0])
    loop(lambda p: sib_copy(0, order(p)).start())

    def first_mix(p):
        g = order(p)
        sib_copy(0, g).wait_recv()
        mix(0, g)
        par_copy(0, g).start()

    loop(first_mix, 0, FIRST)
    hear(known.at[0], rounds[0])
    tell(known.at[1], rounds[1])
    loop(first_mix, FIRST, CHUNKS)
    for copy in small_in:
        copy.wait()
    source_in.wait()
    cross_arrival(0).wait_recv()
    start_planes()
    hear(known.at[1], rounds[1])
    tell(known.at[2], rounds[2])

    def second_mix(p):
        g = order(p)
        sib_copy(1, g).wait_recv()
        mix(1, g)
        par_copy(1, g).start()

    def first_sweep(p):
        g = order(p)

        @pl.when(p == AT_RINGS)
        def _():
            all_done(plane0.at[pl.ds(0, SY - 1)], plane_rsem.at[0])
            forward()
            hear(known.at[2], rounds[2])
            start_rings()
            tell(known.at[3], rounds[3])

        @pl.when(p == AT_HALO_SENDS)
        def _():
            for exists, _ in rounds[3]:

                @pl.when(exists)
                def _():
                    pl.semaphore_wait(known.at[3], 1)

            start_halos(0)

        @pl.when(p == AT_HALOS)
        def _():
            unpack_halos(0)

        par_copy(0, g).wait_recv()
        advance(0, g)
        sib_copy(1, g).start()
        gather(1, g)

        @pl.when(p > 0)
        def _():
            second_mix(p - 1)

    loop(first_sweep)
    turn(1)
    second_mix(CHUNKS - 1)
    all_done(ring0.at[pl.ds(0, SZ - 1)], ring_rsem.at[0])
    settle(0)
    for c in range(2):
        plane1[place, c] = before[c] - pace_lanes[c] * share_lanes[c]
    start_layer()
    start_columns()
    turn_share()
    all_done(sib1, sib_ssem.at[1])
    loop(lambda g: patch(0, g))
    pack_halos(1)
    start_halos(1)
    all_done(plane1.at[pl.ds(0, LAYER - 1)], layer_rsem.at[0])
    pass_across()
    cross_copy(1).start()
    unpack_halos(1)

    def second_sweep(p):
        g = order(p)
        par_copy(1, g).wait_recv()
        advance(1, g)

    loop(second_sweep)
    all_done(columns, column_rsem.at[0])
    cross_arrival(1).wait_recv()
    settle(1)
    turn_share()
    loop(lambda g: patch(1, g))

    all_done(sib0, sib_ssem.at[0])
    all_done(send0, par_ssem.at[0])
    all_done(send1, par_ssem.at[1])
    all_done(columns, column_ssem.at[0])
    all_done(plane0.at[pl.ds(0, SY - 1)], plane_ssem.at[0])
    all_done(ring0.at[pl.ds(0, SZ - 1)], ring_ssem.at[0])
    all_done(plane1.at[pl.ds(0, LAYER - 1)], layer_ssem.at[0])
    for sweep in range(2):
        cross_copy(sweep).wait_send()
        all_done(halos_out[sweep], halo_ssem.at[sweep])


def store(state, resid, state_hbm, resid_hbm, sems):
    copies = [
        pltpu.make_async_copy(state, state_hbm, sems.at[0]),
        pltpu.make_async_copy(resid, resid_hbm, sems.at[1]),
    ]
    for copy in copies:
        copy.start()
    for copy in copies:
        copy.wait()


def local(flow_state, flow_source, pseudo_step, flux_jacobian, stator_donor, stator_weight, rotor_donor, rotor_weight):
    f32 = jnp.float32
    block = (2, NV, ROWS, AX)
    padded = (2, NV, ROWS + 2 * CHUNK, AX)
    chunked = (CHUNKS, 2, NV, CHUNK, AX)
    anywhere = pl.BlockSpec(memory_space=pltpu.HBM)
    vmem = pl.BlockSpec(memory_space=pltpu.VMEM)
    dma = pltpu.SemaphoreType.DMA
    regular = pltpu.SemaphoreType.REGULAR
    halo = (2, 2, NV, AX)
    args = (
        flow_state, flow_source, pseudo_step, flux_jacobian, stator_donor, stator_weight, rotor_donor, rotor_weight
    )
    state, resid = pl.pallas_call(
        kernel,
        out_shape=(pltpu.VMEM(block, f32), pltpu.VMEM(block, f32)),
        in_specs=[anywhere] * 8,
        out_specs=(vmem, vmem),
        scratch_shapes=[
            pltpu.SMEM((NV, NV), f32),
            pltpu.SMEM((2, ROWS), jnp.int32),
            pltpu.VMEM((2, ROWS), f32),
            pltpu.SMEM((2, ROWS), jnp.int32),
            pltpu.VMEM((2, ROWS), f32),
            pltpu.VMEM(padded, f32),
            pltpu.VMEM(padded, f32),
            pltpu.VMEM(block, f32),
            pltpu.VMEM((ROWS, AX), f32),
            *[pltpu.VMEM(chunked, f32) for _ in range(6)],
            pltpu.VMEM((LANES, LANES), f32),
            pltpu.VMEM((SY, SX, 2, NV, LANES), f32),
            pltpu.VMEM((SZ * SY, 2, NV, LANES), f32),
            pltpu.VMEM((SZ, 4, NV, LANES), f32),
            pltpu.VMEM((SX, 4, NV, LANES), f32),
            pltpu.VMEM((3, 2, NV, LANES), f32),
            pltpu.VMEM((2, NV, LANES), f32),
            pltpu.VMEM((2, 1, LANES), f32),
            pltpu.VMEM((2, NV, LANES), f32),
            pltpu.VMEM((LANES, LANES), f32),
            *[pltpu.VMEM(halo, f32) for _ in range(4)],
            regular((4,)),
            dma((8,)),
            dma((2,)),
            dma((2 * CHUNKS,)),
            dma((2,)),
            dma((2 * CHUNKS,)),
            dma((2,)),
            dma((2,)),
            *[dma((1,)) for _ in range(6)],
            dma((2,)),
            dma((2,)),
            dma((1,)),
            dma((1,)),
        ],
        compiler_params=pltpu.CompilerParams(
            collective_id=0, has_side_effects=True, vmem_limit_bytes=24 * 2**20
        ),
    )(*[pltpu.with_memory_space_constraint(arg, pltpu.HBM) for arg in args])
    return pl.pallas_call(
        store,
        out_shape=(pltpu.HBM(block, f32), pltpu.HBM(block, f32)),
        in_specs=[vmem, vmem],
        out_specs=(anywhere, anywhere),
        scratch_shapes=[dma((2,))],
    )(
        pltpu.with_memory_space_constraint(state, pltpu.VMEM), pltpu.with_memory_space_constraint(resid, pltpu.VMEM)
    )


def solution(mesh):
    return jax.shard_map(
        local,
        mesh=mesh,
        in_specs=(
            P("inst", None, "space", None),
            P("inst", None, "space", None),
            P("space", None),
            P(),
            P("inst", "space"),
            P("inst", "space"),
            P("inst", "space"),
            P("inst", "space"),
        ),
        out_specs=(P("inst", None, "space", None), P("inst", None, "space", None)),
        check_vma=False,
    )
```

time: 44.7 us -> 42.5 us (0.951)
  the two profiles are of different devices: /device:TPU:1 before, /device:TPU:8 now
where the time goes in v4:
time: 42.5 us; the launch traced here: 42.4 us
  Pallas kernels  41.7 us (98%)
  between operations  0.64 us (2%)
    pallas_call x1, Pallas kernels, local(): pl.pallas_call(kernel, out_shape=(pltpu.VMEM(block, f32), pltpu.VMEM(bloc...  40.7 us
    pallas_call x1, Pallas kernels, local(): pl.pallas_call(store, out_shape=(pltpu.HBM(block, f32), pltpu.HBM(block,...  1.07 us

profile of v4, /device:TPU:8, one launch (start us, length us, event | category | flops | bytes accessed | tf_op | source)
XLA Modules:
  0.0 42.4 jit_solution(5800482454190672423)
XLA Ops:
  0.6 40.7 %shard_map.95 = (f32[2,5,64,256]{3,2,1,0:T(8,128)S(1)}, f32[2,5,64,256]{3,2,1,0:T(8,128)S(1)}) custom-call(f32[2,5,64,256]{3,2,1,0:T(8,128)} %flow_hbm.1, f32[2,5,64,256]{3,2,1,0:T(8,128)} %source_hbm.1, f32[64,256]{1,0:T(8,128)} %step_hbm.1, f32[5,5]{1,0:T(8,128)} %rest_0_.1, s32[2,64]{1,0:T(2,128)} %rest_1_.1, f32[2,64]{1,0:T(2,128)} %rest_2_.1, ...), custom_call_target="tpu_custom_call" | custom-call | tf_op jit(solution)/shard_map/pallas_call | solution.py:510
  41.3 1.1 %shard_map.96 = (f32[2,5,64,256]{3,2,1,0:T(8,128)}, f32[2,5,64,256]{3,2,1,0:T(8,128)}) custom-call(f32[2,5,64,256]{3,2,1,0:T(8,128)S(1)} %get-tuple-element.4.state, f32[2,5,64,256]{3,2,1,0:T(8,128)S(1)} %get-tuple-element.5.resid), custom_call_target="tpu_custom_call" | custom-call | tf_op jit(solution)/shard_map/pallas_call | solution.py:555

commit v5 on v4

--- a/solution.py
+++ b/solution.py
@@ -19,7 +19,8 @@
 SPACE = SX * SZ * SY
 LAYER = SZ * SY
 VISCOSITY = 0.5
-AT_RINGS, AT_HALO_SENDS, AT_HALOS = 3, 5, 6
+AT_RINGS, AT_HALOS, AT_SETTLE = (3, 1), (5, 3), (6, 5)
+AT_LAYER, AT_SECOND_HALOS = (6, 3), 6
 FIRST = 2
 
 
@@ -41,8 +42,8 @@
     flow_hbm, source_hbm, step_hbm, small_hbm, out_state, out_resid,
     jac, stator_donor, stator_weight, rotor_donor, rotor_weight,
     flow0, flow1, source, step, sib0, sib1, send0, send1, recv0, recv1,
-    corner, plane0, plane1, ring0, cross, columns, before, pace_lanes, share_lanes, share_rows,
-    halo_out0, halo_out1, halo_in0, halo_in1,
+    corner, plane0, plane1, ring0, cross, columns0, columns1, before, pace_lanes, share_lanes, share_rows,
+    halo_out0, halo_out1, halo_in0, halo_in1, relay, relay_sem,
     known, load_sem, sib_ssem, sib_rsem, par_ssem, par_rsem, halo_ssem, halo_rsem,
     plane_ssem, plane_rsem, ring_ssem, ring_rsem, layer_ssem, layer_rsem, cross_ssem, cross_rsem, column_ssem, column_rsem,
 ):
@@ -99,7 +100,7 @@
             count = count + exists.astype(jnp.int32)
         pl.semaphore_wait(semaphore, count)
 
-    rounds = [on_line(1), on_line(2), on_line(4), on_line(SZ - 1)]
+    rounds = [on_line(1), on_line(2), on_line(4)]
     barrier = pltpu.get_barrier_semaphore()
     tell(barrier, nearest)
 
@@ -137,10 +138,37 @@
 
     halos_out, halos_in = (halo_out0, halo_out1), (halo_in0, halo_in1)
 
+    def send_row(sweep, row, into, device):
+        remote(row, into, halo_ssem.at[sweep], halo_rsem.at[sweep], device).start()
+
     def start_halos(sweep):
-        out, into = halos_out[sweep], halos_in[sweep]
-        remote(out.at[0], into.at[1], halo_ssem.at[sweep], halo_rsem.at[sweep], above).start()
-        remote(out.at[1], into.at[0], halo_ssem.at[sweep], halo_rsem.at[sweep], below).start()
+        send_row(sweep, halos_out[sweep].at[0], halos_in[sweep].at[1], above)
+        send_row(sweep, halos_out[sweep].at[1], halos_in[sweep].at[0], below)
+
+    first_in_ring, last_in_ring = y == 0, y == SY - 1
+
+    def start_first_halos():
+        for side, stays, device in ((0, y > 0, above), (1, y < SY - 1, below)):
+
+            @pl.when(stays)
+            def _(side=side, device=device):
+                send_row(0, halo_out0.at[side], halo_in0.at[1 - side], device)
+
+            @pl.when(jnp.logical_not(stays))
+            def _(side=side):
+                other_end = plane_peer(SY - 1 if side == 0 else 1)
+                remote(halo_out0.at[side], relay, halo_ssem.at[0], relay_sem.at[0], other_end).start()
+
+    def pass_halos():
+        for here, side, device in (
+            (last_in_ring, 0, (inst, (space + SPACE - SY) % SPACE)),
+            (first_in_ring, 1, (inst, (space + SY) % SPACE)),
+        ):
+
+            @pl.when(here)
+            def _(side=side, device=device):
+                all_done(relay, relay_sem.at[0])
+                send_row(0, relay, halo_in0.at[1 - side], device)
 
     def pack_halos(sweep):
         flow, out = (flow0 if sweep == 0 else flow1), halos_out[sweep]
@@ -184,35 +212,40 @@
 
         lax.fori_loop(1, LAYER, start, 0)
 
-    def start_columns():
-        mine = plane1.at[place]
+    def start_columns(sweep):
+        mine = plane0.at[y, x] if sweep == 0 else plane1.at[place]
         for k, device in enumerate((sibling, partner, diagonal)):
-            remote(mine, columns.at[k], column_ssem.at[0], column_rsem.at[0], device).start()
-
-    def gather(sweep, g):
-        flow = flow0 if sweep == 0 else flow1
+            into = (columns0, columns1)[sweep].at[k]
+            remote(mine, into, column_ssem.at[sweep], column_rsem.at[sweep], device).start()
+
+    def to_lane(tiles, c, total):
+        for v, tile in enumerate(tiles):
+            q = c * CHUNK + v
+            total = jnp.where(lane == q, pltpu.roll(tile, (q + 1) if c == 0 else q, axis=1), total)
+        return total
+
+    def corner_rows(n, g):
+        return pl.ds(pl.multiple_of(n * ROWS + g * CHUNK, CHUNK), CHUNK)
+
+    def gather(g):
         here = pl.ds(pl.multiple_of(g * CHUNK, CHUNK), CHUNK)
         for n in range(2):
             total = jnp.zeros((CHUNK, LANES), jnp.float32)
             for c in range(2):
                 at = pl.ds(c * LANES, LANES)
-                tiles = [flow[n, v, rows_at(g), at] for v in range(NV)]
-                if sweep == 0:
-                    tiles.append(step[here, at])
-                for v, tile in enumerate(tiles):
-                    q = c * CHUNK + v
-                    total = jnp.where(lane == q, pltpu.roll(tile, (q + 1) if c == 0 else q, axis=1), total)
-            corner[pl.ds(pl.multiple_of(n * ROWS + g * CHUNK, CHUNK), CHUNK), :] = total
-
-    def turn(sweep):
+                total = to_lane([flow0[n, v, rows_at(g), at] for v in range(NV)] + [step[here, at]], c, total)
+            corner[corner_rows(n, g), :] = total
+
+    def turn_first():
         turned = corner[...].T
         for c in range(2):
-            found = turned[c * CHUNK : c * CHUNK + NV, :]
-            if sweep == 0:
-                plane0[y, x, c] = found
-                pace_lanes[c] = turned[c * CHUNK + NV : c * CHUNK + NV + 1, :]
-            else:
-                before[c] = found
+            plane0[y, x, c] = turned[c * CHUNK : c * CHUNK + NV, :]
+            pace_lanes[c] = turned[c * CHUNK + NV : c * CHUNK + NV + 1, :]
+
+    def turn_border():
+        turned = corner[...].T
+        for c in range(2):
+            before[c] = turned[c * CHUNK : c * CHUNK + NV, :]
 
     def donor(c, n):
         return (stator_donor if c == 0 else rotor_donor)[n, 0]
@@ -254,6 +287,7 @@
         return jnp.where(low, here, there)
 
     def settle(sweep):
+        columns = (columns0, columns1)[sweep]
         entering = []
         for c in range(2):
             weights = stator_weight if c == 0 else rotor_weight
@@ -275,16 +309,15 @@
             for w in range(NV):
                 total = total - jac[v, w] * stator[w : w + 1, :]
             share_lanes[1, pl.ds(v, 1), :] = total
-        if sweep == 1:
-            for c in range(2):
-                total = share_lanes[c]
-                for k, table in enumerate((from_sib, to_own, to_sib)):
-                    straight = columns[k, c]
-                    turned = pltpu.roll(straight, ROWS, axis=1)
-                    same = jnp.where(low, table[0][0], table[1][1])
-                    crossed = jnp.where(low, table[0][1], table[1][0])
-                    total = total + (same * straight + crossed * turned)
-                share_lanes[c] = total
+        for c in range(2):
+            total = share_lanes[c]
+            for k, table in enumerate((from_sib, to_own, to_sib)):
+                straight = columns[k, c]
+                turned = pltpu.roll(straight, ROWS, axis=1)
+                same = jnp.where(low, table[0][0], table[1][1])
+                crossed = jnp.where(low, table[0][1], table[1][0])
+                total = total + (same * straight + crossed * turned)
+            share_lanes[c] = total
 
     def turn_share():
         corner[...] = jnp.zeros_like(corner)
@@ -305,40 +338,59 @@
                         + (to_sib[a][0] * other[0] + to_sib[a][1] * other[1])
                     )
 
+    def inner(flow, g, t):
+        here = pl.ds(pl.multiple_of(g * CHUNK, CHUNK), CHUNK)
+        jacobian = [[jac[v, w] for w in range(NV)] for v in range(NV)]
+        at = pl.ds(t * LANES, LANES)
+        centre = [[flow[n, v, rows_at(g), at] for v in range(NV)] for n in range(2)]
+        parts = []
+        for n in range(2):
+            diff, smooth = [], []
+            for v in range(NV):
+                window = flow[n, v, pl.ds(pl.multiple_of(g * CHUNK, CHUNK), 3 * CHUNK), at]
+                upper = window[CHUNK - 1 : 2 * CHUNK - 1]
+                lower = window[CHUNK + 1 : 2 * CHUNK + 1]
+                f = centre[n][v]
+                left = jnp.where(lane == 0, 0.0, pltpu.roll(f, 1, axis=1))
+                right = jnp.where(lane == LANES - 1, 0.0, pltpu.roll(f, LANES - 1, axis=1))
+                diff.append(f - left)
+                smooth.append(VISCOSITY * (4.0 * f - left - right - upper - lower))
+            row = []
+            for v in range(NV):
+                convect = jacobian[v][0] * diff[0]
+                for w in range(1, NV):
+                    convect = convect + jacobian[v][w] * diff[w]
+                derivative = from_own[n][0] * centre[0][v] + from_own[n][1] * centre[1][v]
+                row.append(convect + smooth[v] + derivative - source[n, v, here, at])
+            parts.append(row)
+        return centre, parts
+
+    def border(g):
+        here = pl.ds(pl.multiple_of(g * CHUNK, CHUNK), CHUNK)
+        totals = [jnp.zeros((CHUNK, LANES), jnp.float32) for _ in range(2)]
+        for t in range(2):
+            pace = step[here, pl.ds(t * LANES, LANES)]
+            centre, parts = inner(flow0, g, t)
+            for n in range(2):
+                totals[n] = to_lane([centre[n][v] - pace * parts[n][v] for v in range(NV)], t, totals[n])
+        for n in range(2):
+            corner[corner_rows(n, g), :] = totals[n]
+
     def advance(sweep, g):
         flow, sib, recv = (flow0, sib0, recv0) if sweep == 0 else (flow1, sib1, recv1)
         here = pl.ds(pl.multiple_of(g * CHUNK, CHUNK), CHUNK)
-        jacobian = [[jac[v, w] for w in range(NV)] for v in range(NV)]
         for t in range(2):
             at = pl.ds(t * LANES, LANES)
             pace = step[here, at]
             edge = lane == (LANES - 1 if t == 0 else 0)
-            centre = []
+            centre, parts = inner(flow, g, t)
             for n in range(2):
-                centre.append([flow[n, v, rows_at(g), at] for v in range(NV)])
-            for n in range(2):
-                diff, smooth = [], []
                 for v in range(NV):
-                    window = flow[n, v, pl.ds(pl.multiple_of(g * CHUNK, CHUNK), 3 * CHUNK), at]
-                    upper = window[CHUNK - 1 : 2 * CHUNK - 1]
-                    lower = window[CHUNK + 1 : 2 * CHUNK + 1]
-                    f = centre[n][v]
-                    left = jnp.where(lane == 0, 0.0, pltpu.roll(f, 1, axis=1))
-                    right = jnp.where(lane == LANES - 1, 0.0, pltpu.roll(f, LANES - 1, axis=1))
-                    diff.append(f - left)
-                    smooth.append(VISCOSITY * (4.0 * f - left - right - upper - lower))
-                for v in range(NV):
-                    convect = jacobian[v][0] * diff[0]
-                    for w in range(1, NV):
-                        convect = convect + jacobian[v][w] * diff[w]
                     others = (
                         from_sib[n][0] * sib[g, 0, v, :, at] + from_sib[n][1] * sib[g, 1, v, :, at]
                         + recv[g, n, v, :, at]
                     )
-                    if sweep == 1:
-                        others = jnp.where(edge, 0.0, others)
-                    derivative = from_own[n][0] * centre[0][v] + from_own[n][1] * centre[1][v] + others
-                    residual = convect + smooth[v] + derivative - source[n, v, here, at]
+                    residual = parts[n][v] + jnp.where(edge, 0.0, others)
                     new = centre[n][v] - pace * residual
                     if sweep == 0:
                         flow1[n, v, rows_at(g), at] = new
@@ -349,7 +401,7 @@
     def patch(sweep, g):
         here = pl.ds(pl.multiple_of(g * CHUNK, CHUNK), CHUNK)
         for n in range(2):
-            shares = share_rows[pl.ds(pl.multiple_of(n * ROWS + g * CHUNK, CHUNK), CHUNK), :]
+            shares = share_rows[corner_rows(n, g), :]
             for t in range(2):
                 at = pl.ds(t * LANES, LANES)
                 edge = lane == (LANES - 1 if t == 0 else 0)
@@ -374,11 +426,12 @@
 
     step_in.wait()
     flow_in.wait()
-    loop(lambda g: gather(0, g))
-    turn(0)
+    loop(gather)
+    turn_first()
     pack_halos(0)
     hear(barrier, nearest)
     cross_copy(0).start()
+    start_first_halos()
     tell(known.at[0], rounds[0])
     loop(lambda p: sib_copy(0, order(p)).start())
 
@@ -389,6 +442,7 @@
         par_copy(0, g).start()
 
     loop(first_mix, 0, FIRST)
+    start_columns(0)
     hear(known.at[0], rounds[0])
     tell(known.at[1], rounds[1])
     loop(first_mix, FIRST, CHUNKS)
@@ -399,6 +453,7 @@
     start_planes()
     hear(known.at[1], rounds[1])
     tell(known.at[2], rounds[2])
+    loop(border, 1, CHUNKS - 1)
 
     def second_mix(p):
         g = order(p)
@@ -406,66 +461,74 @@
         mix(1, g)
         par_copy(1, g).start()
 
+    def when(places):
+        low_z, high_z = places
+        return (z < SZ // 2).astype(jnp.int32) * (low_z - high_z) + high_z
+
+    at_rings, at_halos, at_settle, at_layer = (when(a) for a in (AT_RINGS, AT_HALOS, AT_SETTLE, AT_LAYER))
+
     def first_sweep(p):
         g = order(p)
 
-        @pl.when(p == AT_RINGS)
+        @pl.when(p == at_rings)
         def _():
+            hear(known.at[2], rounds[2])
+            pass_halos()
             all_done(plane0.at[pl.ds(0, SY - 1)], plane_rsem.at[0])
             forward()
-            hear(known.at[2], rounds[2])
             start_rings()
-            tell(known.at[3], rounds[3])
-
-        @pl.when(p == AT_HALO_SENDS)
-        def _():
-            for exists, _ in rounds[3]:
-
-                @pl.when(exists)
-                def _():
-                    pl.semaphore_wait(known.at[3], 1)
-
-            start_halos(0)
-
-        @pl.when(p == AT_HALOS)
+
+        @pl.when(p == at_halos)
         def _():
             unpack_halos(0)
+            border(0)
+            border(CHUNKS - 1)
+            turn_border()
+
+        @pl.when(p == at_settle)
+        def _():
+            all_done(ring0.at[pl.ds(0, SZ - 1)], ring_rsem.at[0])
+            all_done(columns0, column_rsem.at[0])
+            settle(0)
+            for c in range(2):
+                plane1[place, c] = before[c] - pace_lanes[c] * share_lanes[c]
+            start_layer()
+            start_columns(1)
+            turn_share()
 
         par_copy(0, g).wait_recv()
         advance(0, g)
         sib_copy(1, g).start()
-        gather(1, g)
 
         @pl.when(p > 0)
         def _():
             second_mix(p - 1)
 
     loop(first_sweep)
-    turn(1)
     second_mix(CHUNKS - 1)
-    all_done(ring0.at[pl.ds(0, SZ - 1)], ring_rsem.at[0])
-    settle(0)
-    for c in range(2):
-        plane1[place, c] = before[c] - pace_lanes[c] * share_lanes[c]
-    start_layer()
-    start_columns()
-    turn_share()
     all_done(sib1, sib_ssem.at[1])
     loop(lambda g: patch(0, g))
     pack_halos(1)
     start_halos(1)
-    all_done(plane1.at[pl.ds(0, LAYER - 1)], layer_rsem.at[0])
-    pass_across()
-    cross_copy(1).start()
-    unpack_halos(1)
 
     def second_sweep(p):
         g = order(p)
+
+        @pl.when(p == at_layer)
+        def _():
+            all_done(plane1.at[pl.ds(0, LAYER - 1)], layer_rsem.at[0])
+            pass_across()
+            cross_copy(1).start()
+
+        @pl.when(p == AT_SECOND_HALOS)
+        def _():
+            unpack_halos(1)
+
         par_copy(1, g).wait_recv()
         advance(1, g)
 
     loop(second_sweep)
-    all_done(columns, column_rsem.at[0])
+    all_done(columns1, column_rsem.at[1])
     cross_arrival(1).wait_recv()
     settle(1)
     turn_share()
@@ -474,13 +537,18 @@
     all_done(sib0, sib_ssem.at[0])
     all_done(send0, par_ssem.at[0])
     all_done(send1, par_ssem.at[1])
-    all_done(columns, column_ssem.at[0])
+    all_done(columns0, column_ssem.at[0])
+    all_done(columns1, column_ssem.at[1])
     all_done(plane0.at[pl.ds(0, SY - 1)], plane_ssem.at[0])
     all_done(ring0.at[pl.ds(0, SZ - 1)], ring_ssem.at[0])
     all_done(plane1.at[pl.ds(0, LAYER - 1)], layer_ssem.at[0])
     for sweep in range(2):
         cross_copy(sweep).wait_send()
         all_done(halos_out[sweep], halo_ssem.at[sweep])
+
+    @pl.when(jnp.logical_or(first_in_ring, last_in_ring))
+    def _():
+        all_done(relay, halo_ssem.at[0])
 
 
 def store(state, resid, state_hbm, resid_hbm, sems):
@@ -528,13 +596,15 @@
             pltpu.VMEM((SZ * SY, 2, NV, LANES), f32),
             pltpu.VMEM((SZ, 4, NV, LANES), f32),
             pltpu.VMEM((SX, 4, NV, LANES), f32),
-            pltpu.VMEM((3, 2, NV, LANES), f32),
+            *[pltpu.VMEM((3, 2, NV, LANES), f32) for _ in range(2)],
             pltpu.VMEM((2, NV, LANES), f32),
             pltpu.VMEM((2, 1, LANES), f32),
             pltpu.VMEM((2, NV, LANES), f32),
             pltpu.VMEM((LANES, LANES), f32),
             *[pltpu.VMEM(halo, f32) for _ in range(4)],
-            regular((4,)),
+            pltpu.VMEM(halo[1:], f32),
+            dma((1,)),
+            regular((3,)),
             dma((8,)),
             dma((2,)),
             dma((2 * CHUNKS,)),
@@ -545,8 +615,8 @@
             *[dma((1,)) for _ in range(6)],
             dma((2,)),
             dma((2,)),
-            dma((1,)),
-            dma((1,)),
+            dma((2,)),
+            dma((2,)),
         ],
         compiler_params=pltpu.CompilerParams(
             collective_id=0, has_side_effects=True, vmem_limit_bytes=24 * 2**20

time: 42.5 us -> 41.7 us (0.981)
  the two profiles are of different devices: /device:TPU:8 before, /device:TPU:1 now
where the time goes in v5:
time: 41.7 us; the launch traced here: 41.6 us
  Pallas kernels  41 us (98%)
  between operations  0.64 us (2%)
    pallas_call x1, Pallas kernels, local(): pl.pallas_call(kernel, out_shape=(pltpu.VMEM(block, f32), pltpu.VMEM(bloc...  39.9 us
    pallas_call x1, Pallas kernels, local(): pl.pallas_call(store, out_shape=(pltpu.HBM(block, f32), pltpu.HBM(block,...  1.07 us

profile of v5, /device:TPU:1, one launch (start us, length us, event | category | flops | bytes accessed | tf_op | source)
XLA Modules:
  0.0 41.6 jit_solution(12958881624604267184)
XLA Ops:
  0.6 39.9 %shard_map.95 = (f32[2,5,64,256]{3,2,1,0:T(8,128)S(1)}, f32[2,5,64,256]{3,2,1,0:T(8,128)S(1)}) custom-call(f32[2,5,64,256]{3,2,1,0:T(8,128)} %flow_hbm.1, f32[2,5,64,256]{3,2,1,0:T(8,128)} %source_hbm.1, f32[64,256]{1,0:T(8,128)} %step_hbm.1, f32[5,5]{1,0:T(8,128)} %rest_0_.1, s32[2,64]{1,0:T(2,128)} %rest_1_.1, f32[2,64]{1,0:T(2,128)} %rest_2_.1, ...), custom_call_target="tpu_custom_call" | custom-call | tf_op jit(solution)/shard_map/pallas_call | solution.py:578
  40.5 1.1 %shard_map.96 = (f32[2,5,64,256]{3,2,1,0:T(8,128)}, f32[2,5,64,256]{3,2,1,0:T(8,128)}) custom-call(f32[2,5,64,256]{3,2,1,0:T(8,128)S(1)} %get-tuple-element.4.state, f32[2,5,64,256]{3,2,1,0:T(8,128)S(1)} %get-tuple-element.5.resid), custom_call_target="tpu_custom_call" | custom-call | tf_op jit(solution)/shard_map/pallas_call | solution.py:625

commit v6 on v5

--- a/solution.py
+++ b/solution.py
@@ -20,7 +20,8 @@
 LAYER = SZ * SY
 VISCOSITY = 0.5
 AT_RINGS, AT_HALOS, AT_SETTLE = (3, 1), (5, 3), (6, 5)
-AT_LAYER, AT_SECOND_HALOS = (6, 3), 6
+AT_LAYER, AT_SECOND_HALOS = (4, 3), 6
+AHEAD, PACE = (5, 3), 3
 FIRST = 2
 
 
@@ -43,7 +44,7 @@
     jac, stator_donor, stator_weight, rotor_donor, rotor_weight,
     flow0, flow1, source, step, sib0, sib1, send0, send1, recv0, recv1,
     corner, plane0, plane1, ring0, cross, columns0, columns1, before, pace_lanes, share_lanes, share_rows,
-    halo_out0, halo_out1, halo_in0, halo_in1, relay, relay_sem,
+    halo_out0, halo_out1, halo_in0, halo_in1, relay, relay_sem, raw, raw_ssem, raw_rsem,
     known, load_sem, sib_ssem, sib_rsem, par_ssem, par_rsem, halo_ssem, halo_rsem,
     plane_ssem, plane_rsem, ring_ssem, ring_rsem, layer_ssem, layer_rsem, cross_ssem, cross_rsem, column_ssem, column_rsem,
 ):
@@ -64,9 +65,6 @@
     def ring_peer(k):
         return inst, x * LAYER + ((z + k) % SZ) * SY + y
 
-    def layer_peer(k):
-        return inst, x * LAYER + (place + k) % LAYER
-
     flow_in = pltpu.make_async_copy(flow_hbm, flow0.at[:, :, pl.ds(CHUNK, ROWS), :], load_sem.at[0])
     source_in = pltpu.make_async_copy(source_hbm, source, load_sem.at[1])
     step_in = pltpu.make_async_copy(step_hbm, step, load_sem.at[2])
@@ -123,6 +121,9 @@
     def rows_at(g):
         return pl.ds(pl.multiple_of(CHUNK + g * CHUNK, CHUNK), CHUNK)
 
+    def order(p):
+        return (p + 1) % CHUNKS
+
     def all_done(ref, semaphore):
         pltpu.make_async_copy(ref, ref, semaphore).wait()
 
@@ -135,6 +136,13 @@
         send, recv = (send0, recv0) if sweep == 0 else (send1, recv1)
         at = sweep * CHUNKS + g
         return remote(send.at[g], recv.at[g], par_ssem.at[sweep], par_rsem.at[at], partner)
+
+    def raw_copy():
+        mine = flow0.at[:, :, rows_at(order(0)), :]
+        return remote(mine, raw.at[0], raw_ssem.at[0], raw_rsem.at[0], partner)
+
+    def raw_pass():
+        return remote(raw.at[0], raw.at[1], raw_ssem.at[1], raw_rsem.at[1], sibling)
 
     halos_out, halos_in = (halo_out0, halo_out1), (halo_in0, halo_in1)
 
@@ -207,10 +215,11 @@
         mine = plane1.at[place]
 
         def start(k, carry):
-            remote(mine, mine, layer_ssem.at[0], layer_rsem.at[0], layer_peer(k)).start()
+            other = k + (k >= place).astype(jnp.int32)
+            remote(mine, mine, layer_ssem.at[0], layer_rsem.at[0], (inst, x * LAYER + other)).start()
             return carry
 
-        lax.fori_loop(1, LAYER, start, 0)
+        lax.fori_loop(0, LAYER - 1, start, 0)
 
     def start_columns(sweep):
         mine = plane0.at[y, x] if sweep == 0 else plane1.at[place]
@@ -286,8 +295,22 @@
         there = cross[((block + 1) // LAYER) % SX, c * 2 + n]
         return jnp.where(low, here, there)
 
-    def settle(sweep):
+    def sum_columns(sweep):
         columns = (columns0, columns1)[sweep]
+        sums = []
+        for c in range(2):
+            total = None
+            for k, table in enumerate((from_sib, to_own, to_sib)):
+                straight = columns[k, c]
+                turned = pltpu.roll(straight, ROWS, axis=1)
+                same = jnp.where(low, table[0][0], table[1][1])
+                crossed = jnp.where(low, table[0][1], table[1][0])
+                term = same * straight + crossed * turned
+                total = term if total is None else total + term
+            sums.append(total)
+        return sums
+
+    def settle(sweep, remote_sum):
         entering = []
         for c in range(2):
             weights = stator_weight if c == 0 else rotor_weight
@@ -310,14 +333,7 @@
                 total = total - jac[v, w] * stator[w : w + 1, :]
             share_lanes[1, pl.ds(v, 1), :] = total
         for c in range(2):
-            total = share_lanes[c]
-            for k, table in enumerate((from_sib, to_own, to_sib)):
-                straight = columns[k, c]
-                turned = pltpu.roll(straight, ROWS, axis=1)
-                same = jnp.where(low, table[0][0], table[1][1])
-                crossed = jnp.where(low, table[0][1], table[1][0])
-                total = total + (same * straight + crossed * turned)
-            share_lanes[c] = total
+            share_lanes[c] = share_lanes[c] + remote_sum[c]
 
     def turn_share():
         corner[...] = jnp.zeros_like(corner)
@@ -325,18 +341,23 @@
             corner[pl.ds(t * CHUNK, NV), :] = share_lanes[t]
         share_rows[...] = corner[...].T
 
-    def mix(sweep, g):
-        flow, sib, send = (flow0, sib0, send0) if sweep == 0 else (flow1, sib1, send1)
+    def spread(own, other, into):
         for v in range(NV):
             for t in range(2):
                 at = pl.ds(t * LANES, LANES)
-                own = [flow[n, v, rows_at(g), at] for n in range(2)]
-                other = [sib[g, n, v, :, at] for n in range(2)]
+                ours, theirs = [own(n, v, at) for n in range(2)], [other(n, v, at) for n in range(2)]
                 for a in range(2):
-                    send[g, a, v, :, at] = (
-                        to_own[a][0] * own[0] + to_own[a][1] * own[1]
-                        + (to_sib[a][0] * other[0] + to_sib[a][1] * other[1])
+                    into[a, v, :, at] = (
+                        to_own[a][0] * ours[0] + to_own[a][1] * ours[1]
+                        + (to_sib[a][0] * theirs[0] + to_sib[a][1] * theirs[1])
                     )
+
+    def mix(sweep, g):
+        flow, sib, send = (flow0, sib0, send0) if sweep == 0 else (flow1, sib1, send1)
+        spread(lambda n, v, at: flow[n, v, rows_at(g), at], lambda n, v, at: sib[g, n, v, :, at], send.at[g])
+
+    def mix_raw():
+        spread(lambda n, v, at: raw[0, n, v, :, at], lambda n, v, at: raw[1, n, v, :, at], recv0.at[order(0)])
 
     def inner(flow, g, t):
         here = pl.ds(pl.multiple_of(g * CHUNK, CHUNK), CHUNK)
@@ -421,9 +442,6 @@
 
         lax.fori_loop(begin, end, wrapped, 0)
 
-    def order(p):
-        return (p + 1) % CHUNKS
-
     step_in.wait()
     flow_in.wait()
     loop(gather)
@@ -431,9 +449,10 @@
     pack_halos(0)
     hear(barrier, nearest)
     cross_copy(0).start()
+    raw_copy().start()
+    loop(lambda p: sib_copy(0, order(p)).start())
+    tell(known.at[0], rounds[0])
     start_first_halos()
-    tell(known.at[0], rounds[0])
-    loop(lambda p: sib_copy(0, order(p)).start())
 
     def first_mix(p):
         g = order(p)
@@ -441,7 +460,7 @@
         mix(0, g)
         par_copy(0, g).start()
 
-    loop(first_mix, 0, FIRST)
+    loop(first_mix, 1, FIRST)
     start_columns(0)
     hear(known.at[0], rounds[0])
     tell(known.at[1], rounds[1])
@@ -454,18 +473,24 @@
     hear(known.at[1], rounds[1])
     tell(known.at[2], rounds[2])
     loop(border, 1, CHUNKS - 1)
+    raw_copy().wait_recv()
+    raw_pass().start()
+
+    def when(places):
+        low_z, high_z = places
+        return (1 - z // (SZ // 2)) * (low_z - high_z) + high_z
+
+    at_rings, at_halos, at_settle, at_layer = (when(a) for a in (AT_RINGS, AT_HALOS, AT_SETTLE, AT_LAYER))
+    ahead = when(AHEAD)
 
     def second_mix(p):
         g = order(p)
         sib_copy(1, g).wait_recv()
         mix(1, g)
-        par_copy(1, g).start()
-
-    def when(places):
-        low_z, high_z = places
-        return (z < SZ // 2).astype(jnp.int32) * (low_z - high_z) + high_z
-
-    at_rings, at_halos, at_settle, at_layer = (when(a) for a in (AT_RINGS, AT_HALOS, AT_SETTLE, AT_LAYER))
+
+        @pl.when(p < ahead)
+        def _():
+            par_copy(1, g).start()
 
     def first_sweep(p):
         g = order(p)
@@ -487,16 +512,26 @@
 
         @pl.when(p == at_settle)
         def _():
+            all_done(columns0, column_rsem.at[0])
+            remote_sum = sum_columns(0)
             all_done(ring0.at[pl.ds(0, SZ - 1)], ring_rsem.at[0])
-            all_done(columns0, column_rsem.at[0])
-            settle(0)
+            settle(0, remote_sum)
             for c in range(2):
                 plane1[place, c] = before[c] - pace_lanes[c] * share_lanes[c]
             start_layer()
             start_columns(1)
             turn_share()
 
-        par_copy(0, g).wait_recv()
+        @pl.when(p == 0)
+        def _():
+            sib_copy(0, g).wait_recv()
+            raw_pass().wait_recv()
+            mix_raw()
+
+        @pl.when(p > 0)
+        def _():
+            par_copy(0, g).wait_recv()
+
         advance(0, g)
         sib_copy(1, g).start()
 
@@ -525,17 +560,25 @@
             unpack_halos(1)
 
         par_copy(1, g).wait_recv()
+
+        @pl.when(jnp.logical_and(p + PACE >= ahead, p + PACE < CHUNKS))
+        def _():
+            par_copy(1, order(p + PACE)).start()
+
         advance(1, g)
 
     loop(second_sweep)
     all_done(columns1, column_rsem.at[1])
+    remote_sum = sum_columns(1)
     cross_arrival(1).wait_recv()
-    settle(1)
+    settle(1, remote_sum)
     turn_share()
     loop(lambda g: patch(1, g))
 
     all_done(sib0, sib_ssem.at[0])
-    all_done(send0, par_ssem.at[0])
+    all_done(send0.at[pl.ds(0, CHUNKS - 1)], par_ssem.at[0])
+    raw_copy().wait_send()
+    raw_pass().wait_send()
     all_done(send1, par_ssem.at[1])
     all_done(columns0, column_ssem.at[0])
     all_done(columns1, column_ssem.at[1])
@@ -604,6 +647,9 @@
             *[pltpu.VMEM(halo, f32) for _ in range(4)],
             pltpu.VMEM(halo[1:], f32),
             dma((1,)),
+            pltpu.VMEM((2, *chunked[1:]), f32),
+            dma((2,)),
+            dma((2,)),
             regular((3,)),
             dma((8,)),
             dma((2,)),

time: 41.7 us -> 39.3 us (0.942)
  Pallas kernels: 41 us -> 38.6 us
    pallas_call x1, Pallas kernels: 39.9 us -> 37.5 us  [local(): pl.pallas_call(kernel, out_shape=(pltpu.VMEM(block, f32), pltpu.VMEM(bloc...]
where the time goes in v6:
time: 39.3 us; the launch traced here: 39.2 us
  Pallas kernels  38.6 us (98%)
  between operations  0.64 us (2%)
    pallas_call x1, Pallas kernels, local(): pl.pallas_call(kernel, out_shape=(pltpu.VMEM(block, f32), pltpu.VMEM(bloc...  37.5 us
    pallas_call x1, Pallas kernels, local(): pl.pallas_call(store, out_shape=(pltpu.HBM(block, f32), pltpu.HBM(block,...  1.07 us

profile of v6, /device:TPU:1, one launch (start us, length us, event | category | flops | bytes accessed | tf_op | source)
XLA Modules:
  0.0 39.2 jit_solution(16855825997128394739)
XLA Ops:
  0.6 37.5 %shard_map.95 = (f32[2,5,64,256]{3,2,1,0:T(8,128)S(1)}, f32[2,5,64,256]{3,2,1,0:T(8,128)S(1)}) custom-call(f32[2,5,64,256]{3,2,1,0:T(8,128)} %flow_hbm.1, f32[2,5,64,256]{3,2,1,0:T(8,128)} %source_hbm.1, f32[64,256]{1,0:T(8,128)} %step_hbm.1, f32[5,5]{1,0:T(8,128)} %rest_0_.1, s32[2,64]{1,0:T(2,128)} %rest_1_.1, f32[2,64]{1,0:T(2,128)} %rest_2_.1, ...), custom_call_target="tpu_custom_call" | custom-call | tf_op jit(solution)/shard_map/pallas_call | solution.py:621
  38.1 1.1 %shard_map.96 = (f32[2,5,64,256]{3,2,1,0:T(8,128)}, f32[2,5,64,256]{3,2,1,0:T(8,128)}) custom-call(f32[2,5,64,256]{3,2,1,0:T(8,128)S(1)} %get-tuple-element.4.state, f32[2,5,64,256]{3,2,1,0:T(8,128)S(1)} %get-tuple-element.5.resid), custom_call_target="tpu_custom_call" | custom-call | tf_op jit(solution)/shard_map/pallas_call | solution.py:671

commit v7 on v6

--- a/solution.py
+++ b/solution.py
@@ -555,6 +555,15 @@
             pass_across()
             cross_copy(1).start()
 
+        @pl.when(p == CHUNKS - 1)
+        def _():
+            all_done(columns1, column_rsem.at[1])
+            remote_sum = sum_columns(1)
+            cross_arrival(1).wait_recv()
+            settle(1, remote_sum)
+            turn_share()
+            loop(lambda g: patch(1, g), 1, CHUNKS)
+
         @pl.when(p == AT_SECOND_HALOS)
         def _():
             unpack_halos(1)
@@ -568,12 +577,7 @@
         advance(1, g)
 
     loop(second_sweep)
-    all_done(columns1, column_rsem.at[1])
-    remote_sum = sum_columns(1)
-    cross_arrival(1).wait_recv()
-    settle(1, remote_sum)
-    turn_share()
-    loop(lambda g: patch(1, g))
+    patch(1, 0)
 
     all_done(sib0, sib_ssem.at[0])
     all_done(send0.at[pl.ds(0, CHUNKS - 1)], par_ssem.at[0])

time: 39.3 us -> 38.7 us (0.985)
  Pallas kernels: 38.6 us -> 38 us
    pallas_call x1, Pallas kernels: 37.5 us -> 36.9 us  [local(): pl.pallas_call(kernel, out_shape=(pltpu.VMEM(block, f32), pltpu.VMEM(bloc...]
where the time goes in v7:
time: 38.7 us; the launch traced here: 38.6 us
  Pallas kernels  38 us (98%)
  between operations  0.64 us (2%)
    pallas_call x1, Pallas kernels, local(): pl.pallas_call(kernel, out_shape=(pltpu.VMEM(block, f32), pltpu.VMEM(bloc...  36.9 us
    pallas_call x1, Pallas kernels, local(): pl.pallas_call(store, out_shape=(pltpu.HBM(block, f32), pltpu.HBM(block,...  1.07 us

profile of v7, /device:TPU:1, one launch (start us, length us, event | category | flops | bytes accessed | tf_op | source)
XLA Modules:
  0.0 38.6 jit_solution(10674804179705617447)
XLA Ops:
  0.6 36.9 %shard_map.95 = (f32[2,5,64,256]{3,2,1,0:T(8,128)S(1)}, f32[2,5,64,256]{3,2,1,0:T(8,128)S(1)}) custom-call(f32[2,5,64,256]{3,2,1,0:T(8,128)} %flow_hbm.1, f32[2,5,64,256]{3,2,1,0:T(8,128)} %source_hbm.1, f32[64,256]{1,0:T(8,128)} %step_hbm.1, f32[5,5]{1,0:T(8,128)} %rest_0_.1, s32[2,64]{1,0:T(2,128)} %rest_1_.1, f32[2,64]{1,0:T(2,128)} %rest_2_.1, ...), custom_call_target="tpu_custom_call" | custom-call | tf_op jit(solution)/shard_map/pallas_call | solution.py:625
  37.5 1.1 %shard_map.96 = (f32[2,5,64,256]{3,2,1,0:T(8,128)}, f32[2,5,64,256]{3,2,1,0:T(8,128)}) custom-call(f32[2,5,64,256]{3,2,1,0:T(8,128)S(1)} %get-tuple-element.4.state, f32[2,5,64,256]{3,2,1,0:T(8,128)S(1)} %get-tuple-element.5.resid), custom_call_target="tpu_custom_call" | custom-call | tf_op jit(solution)/shard_map/pallas_call | solution.py:675

commit v8 on v7

--- a/solution.py
+++ b/solution.py
@@ -21,7 +21,7 @@
 VISCOSITY = 0.5
 AT_RINGS, AT_HALOS, AT_SETTLE = (3, 1), (5, 3), (6, 5)
 AT_LAYER, AT_SECOND_HALOS = (4, 3), 6
-AHEAD, PACE = (5, 3), 3
+AHEAD, PACE = (5, 4), 2
 FIRST = 2
 
 

time: 38.7 us -> 37.9 us (0.979)
  Pallas kernels: 38 us -> 37.2 us
    pallas_call x1, Pallas kernels: 36.9 us -> 36.1 us  [local(): pl.pallas_call(kernel, out_shape=(pltpu.VMEM(block, f32), pltpu.VMEM(bloc...]
where the time goes in v8:
time: 37.9 us; the launch traced here: 37.8 us
  Pallas kernels  37.2 us (98%)
  between operations  0.64 us (2%)
    pallas_call x1, Pallas kernels, local(): pl.pallas_call(kernel, out_shape=(pltpu.VMEM(block, f32), pltpu.VMEM(bloc...  36.1 us
    pallas_call x1, Pallas kernels, local(): pl.pallas_call(store, out_shape=(pltpu.HBM(block, f32), pltpu.HBM(block,...  1.07 us

profile of v8, /device:TPU:1, one launch (start us, length us, event | category | flops | bytes accessed | tf_op | source)
XLA Modules:
  0.0 37.8 jit_solution(14272566504303142423)
XLA Ops:
  0.6 36.1 %shard_map.95 = (f32[2,5,64,256]{3,2,1,0:T(8,128)S(1)}, f32[2,5,64,256]{3,2,1,0:T(8,128)S(1)}) custom-call(f32[2,5,64,256]{3,2,1,0:T(8,128)} %flow_hbm.1, f32[2,5,64,256]{3,2,1,0:T(8,128)} %source_hbm.1, f32[64,256]{1,0:T(8,128)} %step_hbm.1, f32[5,5]{1,0:T(8,128)} %rest_0_.1, s32[2,64]{1,0:T(2,128)} %rest_1_.1, f32[2,64]{1,0:T(2,128)} %rest_2_.1, ...), custom_call_target="tpu_custom_call" | custom-call | tf_op jit(solution)/shard_map/pallas_call | solution.py:625
  36.7 1.1 %shard_map.96 = (f32[2,5,64,256]{3,2,1,0:T(8,128)}, f32[2,5,64,256]{3,2,1,0:T(8,128)}) custom-call(f32[2,5,64,256]{3,2,1,0:T(8,128)S(1)} %get-tuple-element.4.state, f32[2,5,64,256]{3,2,1,0:T(8,128)S(1)} %get-tuple-element.5.resid), custom_call_target="tpu_custom_call" | custom-call | tf_op jit(solution)/shard_map/pallas_call | solution.py:675

commit v9 on v8

--- a/solution.py
+++ b/solution.py
@@ -21,8 +21,8 @@
 VISCOSITY = 0.5
 AT_RINGS, AT_HALOS, AT_SETTLE = (3, 1), (5, 3), (6, 5)
 AT_LAYER, AT_SECOND_HALOS = (4, 3), 6
-AHEAD, PACE = (5, 4), 2
-FIRST = 2
+AHEAD, PACE = (6, 5), 2
+FIRST = 4
 
 
 def spectral(gap):

time: 37.9 us -> 37.9 us (level)
  no operation moved by 1% of the time
where the time goes in v9:
time: 37.9 us; the launch traced here: 37.8 us
  Pallas kernels  37.2 us (98%)
  between operations  0.64 us (2%)
    pallas_call x1, Pallas kernels, local(): pl.pallas_call(kernel, out_shape=(pltpu.VMEM(block, f32), pltpu.VMEM(bloc...  36.1 us
    pallas_call x1, Pallas kernels, local(): pl.pallas_call(store, out_shape=(pltpu.HBM(block, f32), pltpu.HBM(block,...  1.07 us

profile of v9, /device:TPU:1, one launch (start us, length us, event | category | flops | bytes accessed | tf_op | source)
XLA Modules:
  0.0 37.8 jit_solution(14094446436368334752)
XLA Ops:
  0.6 36.1 %shard_map.95 = (f32[2,5,64,256]{3,2,1,0:T(8,128)S(1)}, f32[2,5,64,256]{3,2,1,0:T(8,128)S(1)}) custom-call(f32[2,5,64,256]{3,2,1,0:T(8,128)} %flow_hbm.1, f32[2,5,64,256]{3,2,1,0:T(8,128)} %source_hbm.1, f32[64,256]{1,0:T(8,128)} %step_hbm.1, f32[5,5]{1,0:T(8,128)} %rest_0_.1, s32[2,64]{1,0:T(2,128)} %rest_1_.1, f32[2,64]{1,0:T(2,128)} %rest_2_.1, ...), custom_call_target="tpu_custom_call" | custom-call | tf_op jit(solution)/shard_map/pallas_call | solution.py:625
  36.7 1.1 %shard_map.96 = (f32[2,5,64,256]{3,2,1,0:T(8,128)}, f32[2,5,64,256]{3,2,1,0:T(8,128)}) custom-call(f32[2,5,64,256]{3,2,1,0:T(8,128)S(1)} %get-tuple-element.4.state, f32[2,5,64,256]{3,2,1,0:T(8,128)S(1)} %get-tuple-element.5.resid), custom_call_target="tpu_custom_call" | custom-call | tf_op jit(solution)/shard_map/pallas_call | solution.py:675
